TPU v7x, 128 devices: a whole 4x4x4 slice. The times are simulated.
128 devices in a mesh: dp: 8 (over x_hi, y), tensor: 16 (over z, x_lo, core).
Axes of the slice: x: 4 (x_hi: 2, x_lo: 2; x = x_hi * 2 + x_lo), y: 4, z: 4, core: 2. Of those that a mesh axis runs over, the one named last changes fastest.
Arguments:
- tokens: bfloat16 [16384, 2048], P(('dp', 'tensor')), may hold values from -6 to 6
- segments: int32 [16, 1024], P('dp'), may hold values from 0 to 3, never falling along the last dimension, each value on 1 to 768 neighbouring positions
- first_gain: float32 [2048], P('dp'), may hold values from 0.1 to 1.9
- first_shift: float32 [2048], P('dp'), may hold values from -2 to 2
- heads_weight: float32 [2048, 3, 2048], P('dp', None, 'tensor'), may hold values from -0.125 to 0.125
- heads_bias: float32 [3, 32, 64], P(None, 'tensor', 'dp'), may hold values from -3 to 3
- output_weight: float32 [2048, 2048], P('tensor', 'dp'), may hold values from -1 to 1
- second_gain: float32 [2048], P('dp'), may hold values from 0.1 to 1.9
- second_shift: float32 [2048], P('dp'), may hold values from -2 to 2
- gate_up_weight: float32 [2048, 2, 5632], P('dp', None, 'tensor'), may hold values from -0.125 to 0.125
- down_weight: float32 [5632, 2048], P('tensor', 'dp'), may hold values from -0.078125 to 0.078125
- cotangent: bfloat16 [16384, 2048], P(('dp', 'tensor')), may hold values from -6 to 6
Outputs:
- mixed: float32 [16384, 2048], P(('dp', 'tensor'))
- grad_tokens: float32 [16384, 2048], P(('dp', 'tensor'))
- grad_first_gain: float32 [2048], P(('dp', 'tensor'))
- grad_first_shift: float32 [2048], P(('dp', 'tensor'))
- grad_heads_weight: float32 [2048, 3, 2048], P('dp', None, 'tensor')
- grad_heads_bias: float32 [3, 32, 64], P(None, 'tensor', 'dp')
- grad_output_weight: float32 [2048, 2048], P('tensor', 'dp')
- grad_second_gain: float32 [2048], P(('dp', 'tensor'))
- grad_second_shift: float32 [2048], P(('dp', 'tensor'))
- grad_gate_up_weight: float32 [2048, 2, 5632], P('dp', None, 'tensor')
- grad_down_weight: float32 [5632, 2048], P('tensor', 'dp')
Inputs may be any that keep to these rules, and one draw needn't show every extreme that they name: `segments`: within each sequence of 1024 tokens the segment numbers never fall; each document has 1 to 768 tokens, and one of each sequence has exactly that many.
All inputs are finite; a program needn't handle non-finite values.
Results may differ from a plain program's by a relative error of at most 0.012.
The roundings to bfloat16 on the way count: a program that leaves them out, or rounds other values in their place, can miss the bound.
Values may be sent and summed in bfloat16 or wider, within the bound.
A program may use at most 256 MiB of HBM per device.

v0:
```python
import math

import jax
import jax.numpy as jnp
from jax import lax
from jax.sharding import PartitionSpec as P

D = 2048
HD = 64
ROT = 16
WINDOW = 512
QB = 512
LEN = 1024


NORM_EPS = 1e-05
BASE_FREQ = 10000.0
FAR_NEGATIVE = -1e30


def layer_norm_parts(values):
    centre = values - jnp.mean(values, axis=-1, keepdims=True)
    inverse = lax.rsqrt(jnp.mean(centre * centre, axis=-1, keepdims=True) + NORM_EPS)
    return (centre * inverse, inverse)


def norm_back(upstream, normed, inverse, gain):
    scaled = upstream * gain
    inner = (
        scaled
        - jnp.mean(scaled, axis=-1, keepdims=True)
        - normed * jnp.mean(scaled * normed, axis=-1, keepdims=True)
    )
    return (inner * inverse, jnp.sum(upstream * normed, axis=0), jnp.sum(upstream, axis=0))


def doc_positions(seg_ids):
    length = seg_ids.shape[-1]
    places = jnp.arange(length, dtype=jnp.int32)
    is_start = jnp.concatenate(
        [
            jnp.ones_like(seg_ids[..., :1]),
            (seg_ids[..., 1:] != seg_ids[..., :-1]).astype(jnp.int32),
        ],
        axis=-1,
    )
    starts = lax.cummax(jnp.where(is_start > 0, places, 0), axis=seg_ids.ndim - 1)
    return places - starts


def rotate(values, places, sign):
    half_rot = ROT // 2
    inverse = jnp.exp(jnp.arange(half_rot, dtype=jnp.float32) * (-2.0 * math.log(BASE_FREQ) / ROT))
    angles = places.astype(jnp.float32)[..., None] * inverse
    cosine = jnp.cos(angles)[..., None, :]
    sine_part = sign * jnp.sin(angles)[..., None, :]
    first_half = values[..., :half_rot]
    second_half = values[..., half_rot:ROT]
    return jnp.concatenate(
        [
            first_half * cosine - second_half * sine_part,
            second_half * cosine + first_half * sine_part,
            values[..., ROT:],
        ],
        axis=-1,
    )


def matmul_nt(left, right):
    return lax.dot_general(
        left, right, (((1,), (1,)), ((), ())), preferred_element_type=jnp.float32
    )


def matmul_tn(left, right):
    return lax.dot_general(
        left, right, (((0,), (0,)), ((), ())), preferred_element_type=jnp.float32
    )


def pad_front(array, seq_count):
    shaped = array.reshape((seq_count, LEN) + array.shape[1:])
    return jnp.concatenate(
        [jnp.zeros((seq_count, QB) + array.shape[1:], array.dtype), shaped], axis=1
    )


def key_window(padded, sequence, local_block):
    one_line = lax.dynamic_index_in_dim(padded, sequence, 0, keepdims=False)
    return lax.dynamic_slice_in_dim(one_line, local_block * QB, 2 * QB, 0)


def add_window(padded, update, sequence, local_block):
    one_line = lax.dynamic_index_in_dim(padded, sequence, 0, keepdims=False)
    window = lax.dynamic_slice_in_dim(one_line, local_block * QB, 2 * QB, 0) + update
    one_line = lax.dynamic_update_slice_in_dim(one_line, window, local_block * QB, 0)
    return lax.dynamic_update_index_in_dim(padded, one_line, sequence, 0)


def window_mask(seg_pad, sequence, local_block):
    first_row = local_block * QB
    row_ids = first_row + jnp.arange(QB, dtype=jnp.int32)
    col_ids = first_row - QB + jnp.arange(2 * QB, dtype=jnp.int32)
    distance = row_ids[:, None] - col_ids[None, :]
    in_window = (distance >= 0) & (distance < WINDOW)
    one_line = lax.dynamic_index_in_dim(seg_pad, sequence, 0, keepdims=False)
    seg_rows = lax.dynamic_slice_in_dim(one_line, first_row + QB, QB, 0)
    seg_cols = lax.dynamic_slice_in_dim(one_line, first_row, 2 * QB, 0)
    return in_window & (seg_rows[:, None] == seg_cols[None, :])


def per_device(
    tokens,
    segments,
    first_gain,
    first_shift,
    heads_weight,
    heads_bias,
    output_weight,
    second_gain,
    second_shift,
    gate_up_weight,
    down_weight,
    cotangent,
):
    (
        heads_full,
        output_full,
        gate_up_full,
        down_full,
        gain_low,
        shift_low,
        bias_low,
        gain_low_two,
        shift_low_two,
    ) = (
        lax.all_gather(heads_weight.astype(jnp.bfloat16), "dp", axis=0, tiled=True),
        lax.all_gather(output_weight.astype(jnp.bfloat16), "dp", axis=1, tiled=True),
        lax.all_gather(gate_up_weight.astype(jnp.bfloat16), "dp", axis=0, tiled=True),
        lax.all_gather(down_weight.astype(jnp.bfloat16), "dp", axis=1, tiled=True),
        lax.all_gather(first_gain.astype(jnp.bfloat16), "dp", axis=0, tiled=True),
        lax.all_gather(first_shift.astype(jnp.bfloat16), "dp", axis=0, tiled=True),
        lax.all_gather(heads_bias.astype(jnp.bfloat16), "dp", axis=2, tiled=True),
        lax.all_gather(second_gain.astype(jnp.bfloat16), "dp", axis=0, tiled=True),
        lax.all_gather(second_shift.astype(jnp.bfloat16), "dp", axis=0, tiled=True),
    )
    gain_one = gain_low.astype(jnp.float32)
    shift_one = shift_low.astype(jnp.float32)
    gain_two = gain_low_two.astype(jnp.float32)
    shift_two = shift_low_two.astype(jnp.float32)
    bias_full = bias_low.astype(jnp.float32)
    head_local = bias_full.shape[1]
    width_local = head_local * HD
    ffn_local = gate_up_full.shape[2]
    own_rows = tokens.shape[0]
    own_start = lax.axis_index("tensor") * own_rows
    seq_count = segments.shape[0]
    all_rows = seq_count * LEN
    per_seq = LEN // QB
    block_count = all_rows // QB
    head_scale = HD ** (-0.5)
    places = doc_positions(segments).reshape(all_rows)
    seg_pad = jnp.concatenate([jnp.full((seq_count, QB), -1, jnp.int32), segments], axis=1)
    inputs = tokens.astype(jnp.float32)
    normed_one, inverse_one = layer_norm_parts(inputs)
    first_low = (normed_one * gain_one + shift_one).astype(jnp.bfloat16)
    carried = (first_low, tokens)
    gathered = (
        lax.all_gather(carried[0], "tensor", axis=0, tiled=True),
        lax.all_gather(carried[1], "tensor", axis=0, tiled=True),
    )
    first_all = gathered[0]
    projected = jnp.dot(
        first_all, heads_full.reshape(D, 3 * width_local), preferred_element_type=jnp.float32
    ) + bias_full.reshape(-1)
    projected = projected.reshape(all_rows, 3, head_local, HD)
    query = (rotate(projected[:, 0], places, 1.0) * head_scale).astype(jnp.bfloat16)
    keys = rotate(projected[:, 1], places, 1.0).astype(jnp.bfloat16)
    values = projected[:, 2].astype(jnp.bfloat16)
    key_pad = pad_front(keys, seq_count)
    value_pad = pad_front(values, seq_count)

    def block_inputs(block_id):
        sequence = block_id // per_seq
        local_block = block_id % per_seq
        q_block = lax.dynamic_slice_in_dim(query, block_id * QB, QB, 0)
        k_block = key_window(key_pad, sequence, local_block)
        v_block = key_window(value_pad, sequence, local_block)
        allowed = window_mask(seg_pad, sequence, local_block)
        scores = jnp.einsum("qhd,khd->hqk", q_block, k_block, preferred_element_type=jnp.float32)
        return (
            q_block,
            k_block,
            v_block,
            jnp.where(allowed[None], scores, FAR_NEGATIVE),
            sequence,
            local_block,
        )

    def attend_block(block_id):
        q_block, k_block, v_block, scores, sequence, local_block = block_inputs(block_id)
        maxima = jnp.max(scores, axis=-1, keepdims=True)
        weights = jnp.exp(scores - maxima)
        totals = jnp.sum(weights, axis=-1, keepdims=True)
        probabilities = weights / totals
        output_block = jnp.einsum(
            "hqk,khd->qhd",
            probabilities.astype(jnp.bfloat16),
            v_block,
            preferred_element_type=jnp.float32,
        )
        return (output_block, maxima, totals)

    block_ids = jnp.arange(block_count, dtype=jnp.int32)
    attn_blocks, maxima_all, totals_all = lax.map(attend_block, block_ids)
    attended = attn_blocks.reshape(all_rows, width_local).astype(jnp.bfloat16)
    attn_full = lax.psum(
        jnp.dot(attended, output_full, preferred_element_type=jnp.float32), "tensor"
    )
    residual_all = gathered[1].astype(jnp.float32) + attn_full
    normed_all, inverse_all = layer_norm_parts(residual_all)
    second_all = (normed_all * gain_two + shift_two).astype(jnp.bfloat16)
    residual = lax.dynamic_slice_in_dim(residual_all, own_start, own_rows, 0)
    normed_two = lax.dynamic_slice_in_dim(normed_all, own_start, own_rows, 0)
    inverse_two = lax.dynamic_slice_in_dim(inverse_all, own_start, own_rows, 0)
    second_low = lax.dynamic_slice_in_dim(second_all, own_start, own_rows, 0)
    gate_up = jnp.dot(
        second_all, gate_up_full.reshape(D, 2 * ffn_local), preferred_element_type=jnp.float32
    ).reshape(all_rows, 2, ffn_local)
    gate_pre = gate_up[:, 0]
    up_pre = gate_up[:, 1]
    sigmoid_gate = jax.nn.sigmoid(gate_pre)
    silu_gate = gate_pre * sigmoid_gate
    hidden = (silu_gate * up_pre).astype(jnp.bfloat16)
    mixed = residual + lax.psum_scatter(
        jnp.dot(hidden, down_full, preferred_element_type=jnp.float32),
        "tensor",
        scatter_dimension=0,
        tiled=True,
    )
    back_heads, back_output, back_gate_up, back_down = (
        lax.all_gather(heads_weight.astype(jnp.bfloat16), "dp", axis=0, tiled=True),
        lax.all_gather(output_weight.astype(jnp.bfloat16), "dp", axis=1, tiled=True),
        lax.all_gather(gate_up_weight.astype(jnp.bfloat16), "dp", axis=0, tiled=True),
        lax.all_gather(down_weight.astype(jnp.bfloat16), "dp", axis=1, tiled=True),
    )
    back_heads_flat = back_heads.reshape(D, 3 * width_local)
    back_gate_up_flat = back_gate_up.reshape(D, 2 * ffn_local)
    upstream = cotangent.astype(jnp.float32)
    up_all = lax.all_gather(cotangent, "tensor", axis=0, tiled=True)
    hidden_grad = matmul_nt(up_all, back_down)
    grad_down = matmul_tn(hidden, up_all)
    gate_grad = hidden_grad * up_pre * sigmoid_gate * (1.0 + gate_pre * (1.0 - sigmoid_gate))
    up_grad = hidden_grad * silu_gate
    gate_up_grad = (
        jnp.stack([gate_grad, up_grad], axis=1)
        .astype(jnp.bfloat16)
        .reshape(all_rows, 2 * ffn_local)
    )
    grad_gate_up = matmul_tn(lax.all_gather(second_low, "tensor", axis=0, tiled=True), gate_up_grad)
    second_grad = lax.psum_scatter(
        matmul_nt(gate_up_grad, back_gate_up_flat), "tensor", scatter_dimension=0, tiled=True
    )
    residual_part, grad_gain_two, grad_shift_two = norm_back(
        second_grad, normed_two, inverse_two, gain_two
    )
    residual_grad = upstream + residual_part
    branch_all = lax.all_gather(residual_grad.astype(jnp.bfloat16), "tensor", axis=0, tiled=True)
    attended_grad = (
        matmul_nt(branch_all, back_output).astype(jnp.bfloat16).reshape(all_rows, head_local, HD)
    )
    grad_output = matmul_tn(attended, branch_all)

    def back_block(carry, block_id):
        key_acc, value_acc = carry
        q_block, k_block, v_block, scores, sequence, local_block = block_inputs(block_id)
        probabilities = jnp.exp(scores - maxima_all[block_id]) / totals_all[block_id]
        grad_block = lax.dynamic_slice_in_dim(attended_grad, block_id * QB, QB, 0)
        prob_grad = jnp.einsum(
            "qhd,khd->hqk", grad_block, v_block, preferred_element_type=jnp.float32
        )
        row_inner = jnp.sum(probabilities * prob_grad, axis=-1, keepdims=True)
        score_grad = (probabilities * (prob_grad - row_inner)).astype(jnp.bfloat16)
        query_grad = jnp.einsum(
            "hqk,khd->qhd", score_grad, k_block, preferred_element_type=jnp.float32
        )
        key_grad = jnp.einsum(
            "hqk,qhd->khd", score_grad, q_block, preferred_element_type=jnp.float32
        )
        value_grad = jnp.einsum(
            "hqk,qhd->khd",
            probabilities.astype(jnp.bfloat16),
            grad_block,
            preferred_element_type=jnp.float32,
        )
        key_acc = add_window(key_acc, key_grad, sequence, local_block)
        value_acc = add_window(value_acc, value_grad, sequence, local_block)
        return ((key_acc, value_acc), query_grad)

    zero_pad = jnp.zeros((seq_count, QB + LEN, head_local, HD), jnp.float32)
    (key_acc, value_acc), query_grads = lax.scan(back_block, (zero_pad, zero_pad), block_ids)
    query_grads = query_grads.reshape(all_rows, head_local, HD)
    keys_grad = key_acc[:, QB:].reshape(all_rows, head_local, HD)
    values_grad = value_acc[:, QB:].reshape(all_rows, head_local, HD)
    projected_grad = jnp.stack(
        [
            rotate(query_grads * head_scale, places, -1.0),
            rotate(keys_grad, places, -1.0),
            values_grad,
        ],
        axis=1,
    )
    projected_grad = projected_grad.astype(jnp.bfloat16).reshape(all_rows, 3 * width_local)
    grad_bias = jnp.sum(projected_grad.astype(jnp.float32), axis=0).reshape(3, head_local, HD)
    grad_heads = matmul_tn(lax.all_gather(first_low, "tensor", axis=0, tiled=True), projected_grad)
    first_grad = lax.psum_scatter(
        matmul_nt(projected_grad, back_heads_flat), "tensor", scatter_dimension=0, tiled=True
    )
    input_part, grad_gain_one, grad_shift_one = norm_back(
        first_grad, normed_one, inverse_one, gain_one
    )
    grad_tokens = residual_grad + input_part
    summed_heads, summed_bias, summed_output, summed_gate_up, summed_down = (
        lax.psum_scatter(
            grad_heads.reshape(D, 3, width_local), "dp", scatter_dimension=0, tiled=True
        ),
        lax.psum_scatter(grad_bias, "dp", scatter_dimension=2, tiled=True),
        lax.psum_scatter(grad_output, "dp", scatter_dimension=1, tiled=True),
        lax.psum_scatter(
            grad_gate_up.reshape(D, 2, ffn_local), "dp", scatter_dimension=0, tiled=True
        ),
        lax.psum_scatter(grad_down, "dp", scatter_dimension=1, tiled=True),
    )
    norm_gain_one, norm_shift_one, norm_gain_two, norm_shift_two = (
        lax.psum_scatter(grad_gain_one, ("dp", "tensor"), scatter_dimension=0, tiled=True),
        lax.psum_scatter(grad_shift_one, ("dp", "tensor"), scatter_dimension=0, tiled=True),
        lax.psum_scatter(grad_gain_two, ("dp", "tensor"), scatter_dimension=0, tiled=True),
        lax.psum_scatter(grad_shift_two, ("dp", "tensor"), scatter_dimension=0, tiled=True),
    )
    return (
        mixed,
        grad_tokens,
        norm_gain_one,
        norm_shift_one,
        summed_heads,
        summed_bias,
        summed_output,
        norm_gain_two,
        norm_shift_two,
        summed_gate_up,
        summed_down,
    )


def solution(mesh):
    return jax.shard_map(
        per_device,
        mesh=mesh,
        in_specs=(
            P(("dp", "tensor"), None),
            P("dp", None),
            P("dp"),
            P("dp"),
            P("dp", None, "tensor"),
            P(None, "tensor", "dp"),
            P("tensor", "dp"),
            P("dp"),
            P("dp"),
            P("dp", None, "tensor"),
            P("tensor", "dp"),
            P(("dp", "tensor"), None),
        ),
        out_specs=(
            P(("dp", "tensor"), None),
            P(("dp", "tensor"), None),
            P(("dp", "tensor")),
            P(("dp", "tensor")),
            P("dp", None, "tensor"),
            P(None, "tensor", "dp"),
            P("tensor", "dp"),
            P(("dp", "tensor")),
            P(("dp", "tensor")),
            P("dp", None, "tensor"),
            P("tensor", "dp"),
        ),
        check_vma=False,
    )
```

profile of v0, /device:TPU:0, one launch (start us, length us, event | category | flops | bytes accessed | tf_op | source)
XLA Modules:
  0.0 1761.0 jit_solution(16761498027645838033)
XLA Ops:
  10.5 23.6 %all-gather.1 = bf16[8,1,256]{2,1,0:T(2,128)(2,1)S(1)} all-gather(bf16[1,1,256]{2,1,0:T(2,128)(2,1)S(1)} %reshape.468), channel_id=1, replica_groups=mesh['dp'=8,'tensor'=16] {'dp'}, dimensions={0}, use_global_device_ids=true | all-gather | bytes 4608 | tf_op jit(solution)/shard_map/all_gather | solution.py:142
  34.2 18.1 %all-gather = bf16[8,1,256]{2,1,0:T(2,128)(2,1)S(1)} all-gather(bf16[1,1,256]{2,1,0:T(2,128)(2,1)S(1)} %reshape.466), channel_id=1, replica_groups=mesh['dp'=8,'tensor'=16] {'dp'}, dimensions={0}, use_global_device_ids=true | all-gather | bytes 4608 | tf_op jit(solution)/shard_map/all_gather | solution.py:141
  59.8 34.1 %all_gather.52 = bf16[3,2,64]{0,1,2:T(2,128)(2,1)S(1)} all-gather(bf16[3,2,8]{0,1,2:T(2,128)(2,1)S(1)} %copy.58), channel_id=1, replica_groups=mesh['dp'=8,'tensor'=16] {'dp'}, dimensions={2}, use_global_device_ids=true | all-gather | bytes 864 | tf_op jit(solution)/shard_map/all_gather | solution.py:143
  95.0 38.2 %all_gather.53 = bf16[128,2048]{1,0:T(8,128)(2,1)} all-gather(bf16[128,256]{1,0:T(8,128)(2,1)S(1)} %convert_element_type.156), channel_id=1, replica_groups=mesh['dp'=8,'tensor'=16] {'dp'}, dimensions={1}, use_global_device_ids=true | all-gather | bytes 589824 | tf_op jit(solution)/shard_map/all_gather | solution.py:138
  153.0 40.8 %while.36 = (s32[]{:T(128)}, bf16[4,512,2,64]{1,3,2,0:T(8,128)(2,1)}, f32[4,2,512,1]{2,1,3,0:T(2,128)S(1)}, f32[4,2,512,1]{2,1,3,0:T(2,128)S(1)}, s32[4]{0:T(128...) while((s32[]{:T(128)}, ...), condition=%wide.region_7.8_spmd.clone, body=%wide.region_4.7_spmd.sunk.clone | while | flops 281017888 | bytes 19860088 | solution.py:215
  208.3 20.0 %all-gather.3 = bf16[8,1,256]{2,1,0:T(2,128)(2,1)S(1)} all-gather(bf16[1,1,256]{2,1,0:T(2,128)(2,1)S(1)} %reshape.472), channel_id=1, replica_groups=mesh['dp'=8,'tensor'=16] {'dp'}, dimensions={0}, use_global_device_ids=true | all-gather | bytes 4608 | tf_op jit(solution)/shard_map/all_gather | solution.py:145
  228.3 19.4 %all-gather.2 = bf16[8,1,256]{2,1,0:T(2,128)(2,1)S(1)} all-gather(bf16[1,1,256]{2,1,0:T(2,128)(2,1)S(1)} %reshape.470), channel_id=1, replica_groups=mesh['dp'=8,'tensor'=16] {'dp'}, dimensions={0}, use_global_device_ids=true | all-gather | bytes 4608 | tf_op jit(solution)/shard_map/all_gather | solution.py:144
  247.8 319.6 %all-reduce.12.cloned.1.call-done = f32[2048,2048]{1,0:T(8,128)} async-done(((f32[2048,2048]{1,0:T(8,128)}), f32[2048,2048]{1,0:T(8,128)}) %all-reduce.12.cloned.1.call-update) | async-done | bytes 16777232 | tf_op jit(solution)/shard_map/psum | solution.py:217
  567.4 14.6 fusion.76
  589.5 15.9 add_convert_fusion
  605.4 24.6 %all-gather.19.cloned.1.call-done = bf16[2048,2,352]{0,2,1:T(8,128)(2,1)} async-done(((bf16[256,2,352]{0,2,1:T(8,128)(2,1)}), bf16[2048,2,352]{0,2,1:T(8,128)(2,1)}) %all-gather.19.cloned.1.call-update) | async-done | bytes 2883600 | tf_op jit(solution)/shard_map/all_gather | solution.py:139
  630.1 11.1 fusion.51
  641.2 38.0 %all-gather.21.cloned.1.call-done = bf16[352,2048]{1,0:T(8,128)(2,1)} async-done(((bf16[352,256]{1,0:T(8,128)(2,1)}), bf16[352,2048]{1,0:T(8,128)(2,1)}) %all-gather.21.cloned.1.call-update) | async-done | bytes 1441808 | tf_op jit(solution)/shard_map/all_gather | solution.py:140
  679.2 51.8 %all-gather.23.cloned.1.call-done = bf16[2048,2048]{1,0:T(8,128)(2,1)} async-done(((bf16[128,2048]{1,0:T(8,128)(2,1)}), bf16[2048,2048]{1,0:T(8,128)(2,1)}) %all-gather.23.cloned.1.call-update) | async-done | bytes 8388624 | tf_op jit(solution)/shard_map/all_gather | solution.py:250
  752.9 183.5 %reduce-scatter.11.cloned.1.call-done = f32[128,2048]{1,0:T(8,128)} async-done(((f32[2048,2048]{1,0:T(8,128)}), f32[128,2048]{1,0:T(8,128)}) %reduce-scatter.11.cloned.1.call-update) | async-done | bytes 1048592 | tf_op jit(solution)/shard_map/reduce_scatter | solution.py:261
  956.7 35.6 %all-gather.25.cloned.1.call-done = bf16[2048,2048]{1,0:T(8,128)(2,1)} async-done(((bf16[128,2048]{1,0:T(8,128)(2,1)}), bf16[2048,2048]{1,0:T(8,128)(2,1)}) %all-gather.25.cloned.1.call-update) | async-done | bytes 8388624 | tf_op jit(solution)/shard_map/all_gather | solution.py:268
  1000.9 79.9 %while.37 = (s32[]{:T(128)}, f32[2,1536,2,64]{1,3,2,0:T(8,128)S(1)}, f32[2,1536,2,64]{1,3,2,0:T(8,128)}, f32[4,512,2,64]{1,3,2,0:T(8,128)}, s32[4]{0:T(128)S(1)}...) while((s32[]{:T(128)}, ...), condition=%wide.region_17.18_spmd.clone, body=%wide.region_15.17_spmd.sunk.clone | while | flops 683934208 | bytes 38337180 | solution.py:301
  1135.8 97.1 %reduce-scatter.9.cloned.1.call-done = f32[128,2048]{1,0:T(8,128)} async-done(((f32[2048,2048]{1,0:T(8,128)}), f32[128,2048]{1,0:T(8,128)}) %reduce-scatter.9.cloned.1.call-update) | async-done | bytes 1048592 | tf_op jit(solution)/shard_map/reduce_scatter | solution.py:235
  1235.6 24.0 %all-reduce.6 = f32[3,2,64]{2,1,0:T(2,128)S(1)} all-reduce(f32[3,2,64]{2,1,0:T(2,128)S(1)} %get-tuple-element.529), channel_id=8, replica_groups=mesh['dp'=8,'tensor'=16] {'dp'}, use_global_device_ids=true, to_apply=%region_27.28.clone | all-reduce | flops 384 | bytes 3072
  1260.2 156.2 %reduce-scatter.13.cloned.1.call-done = f32[128,2048]{1,0:T(8,128)} async-done(((f32[2048,2048]{1,0:T(8,128)}), f32[128,2048]{1,0:T(8,128)}) %reduce-scatter.13.cloned.1.call-update) | async-done | bytes 1048592 | tf_op jit(solution)/shard_map/reduce_scatter | solution.py:316
  1418.2 68.3 %all-reduce.9 = (f32[2048]{0:T(1024)S(1)}, f32[2048]{0:T(1024)S(1)}, f32[2048]{0:T(1024)S(1)}, f32[2048]{0:T(1024)S(1)}) all-reduce(f32[2048]{0:T(1024)S(1)} %get-tuple-element.477, f32[2048]{0:T(1024)S(1)} %get-tuple-element.482, f32[2048]{0:T(1024)S(1)} %get-tuple-element.475, ...), channel_id=5, replica_groups=mesh['dp'=8,'tensor'=16] {'dp','tensor'}, use_global_device_ids=true, to_apply=%region_22.23.clone | all-reduce | flops 8192 | bytes 65536
  1498.1 98.1 %reduce-scatter.19.cloned.1.call-done = f32[256,2,352]{0,2,1:T(8,128)} async-done(((f32[2048,2,352]{0,2,1:T(8,128)}), f32[256,2,352]{0,2,1:T(8,128)}) %reduce-scatter.19.cloned.1.call-update) | async-done | bytes 720912 | tf_op jit(solution)/shard_map/reduce_scatter | solution.py:329
  1596.2 74.3 %reduce-scatter.17.cloned.1.call-done = f32[128,256]{1,0:T(8,128)} async-done(((f32[128,2048]{1,0:T(8,128)}), f32[128,256]{1,0:T(8,128)}) %reduce-scatter.17.cloned.1.call-update) | async-done | bytes 131088 | tf_op jit(solution)/shard_map/reduce_scatter | solution.py:328
  1670.4 83.6 %reduce-scatter.15.cloned.1.call-done = f32[256,3,128]{2,0,1:T(8,128)} async-done(((f32[2048,3,128]{2,0,1:T(8,128)}), f32[256,3,128]{2,0,1:T(8,128)}) %reduce-scatter.15.cloned.1.call-update) | async-done | bytes 393232 | tf_op jit(solution)/shard_map/reduce_scatter | solution.py:324
  (332 shorter events, 263.5 us)
Async XLA Ops:
  7.2 51.4 %copy-start.24 = (s32[2,1024]{1,0:T(2,128)S(1)}, s32[2,1024]{1,0:T(2,128)}, u32[]{:S(2)}) copy-start(s32[2,1024]{1,0:T(2,128)} %param.17) | copy-start | bytes 24580
  7.2 86.8 %copy-start.23 = (f32[128,256]{1,0:T(8,128)S(1)}, f32[128,256]{1,0:T(8,128)}, u32[]{:S(2)}) copy-start(f32[128,256]{1,0:T(8,128)} %param.22) | copy-start | bytes 393220
  7.2 126.9 %all-gather.17.cloned.1.call-start = ((), (), s32[]{:S(2)}) async-start(), calls=%async_computation.9 | async-start | bytes 1769472 | tf_op jit(solution)/shard_map/all_gather | solution.py:137
  9.1 125.0 %all-gather.15.cloned.1.call-start = ((), (), s32[]{:S(2)}) async-start(), calls=%async_computation.8 | async-start | bytes 8912896 | tf_op jit(solution)/shard_map/all_gather | solution.py:169
  57.7 190.1 %all-gather.13.cloned.1.call-start = ((), (), s32[]{:S(2)}) async-start(), calls=%async_computation.7 | async-start | bytes 8912896 | tf_op jit(solution)/shard_map/all_gather | solution.py:170
  58.4 509.0 %all-reduce.12.cloned.1.call-start = ((), (), s32[]{:S(2)}) async-start(), calls=%async_computation.10 | async-start | bytes 33554432 | tf_op jit(solution)/shard_map/psum | solution.py:217
  204.8 425.2 %all-gather.19.cloned.1.call-start = ((), (), s32[]{:S(2)}) async-start(), calls=%async_computation.11 | async-start | bytes 3244032 | tf_op jit(solution)/shard_map/all_gather | solution.py:139
  206.7 472.5 %all-gather.21.cloned.1.call-start = ((), (), s32[]{:S(2)}) async-start(), calls=%async_computation.12 | async-start | bytes 1622016 | tf_op jit(solution)/shard_map/all_gather | solution.py:140
  207.4 523.6 %all-gather.23.cloned.1.call-start = ((), (), s32[]{:S(2)}) async-start(), calls=%async_computation.14 | async-start | bytes 8912896 | tf_op jit(solution)/shard_map/all_gather | solution.py:250
  208.2 728.2 %reduce-scatter.11.cloned.1.call-start = ((), (), s32[]{:S(2)}) async-start(), calls=%async_computation.15 | async-start | bytes 17825792 | tf_op jit(solution)/shard_map/reduce_scatter | solution.py:261
  752.7 185.6 %copy-start.11 = (bf16[128,2048]{1,0:T(8,128)(2,1)S(1)}, bf16[128,2048]{1,0:T(8,128)(2,1)}, u32[]{:S(2)}) copy-start(bf16[128,2048]{1,0:T(8,128)(2,1)} %param.27) | copy-start | bytes 1572868
  752.8 239.5 %all-gather.25.cloned.1.call-start = ((), (), s32[]{:S(2)}) async-start(), calls=%async_computation.16 | async-start | bytes 8912896 | tf_op jit(solution)/shard_map/all_gather | solution.py:268
  941.4 165.3 %all-gather.27.cloned.1.call-start = ((), (), s32[]{:S(2)}) async-start(), calls=%async_computation.20 | async-start | bytes 8912896 | tf_op jit(solution)/shard_map/all_gather | solution.py:260
  943.3 289.6 %reduce-scatter.9.cloned.1.call-start = ((), (), s32[]{:S(2)}) async-start(), calls=%async_computation.13 | async-start | bytes 17825792 | tf_op jit(solution)/shard_map/reduce_scatter | solution.py:235
  956.7 459.8 %reduce-scatter.13.cloned.1.call-start = ((), (), s32[]{:S(2)}) async-start(), calls=%async_computation.17 | async-start | bytes 17825792 | tf_op jit(solution)/shard_map/reduce_scatter | solution.py:316
  1097.0 401.0 %reduce-scatter.21.cloned.1.call-start = ((), (), s32[]{:S(2)}) async-start(), calls=%async_computation.22 | async-start | bytes 3244032 | tf_op jit(solution)/shard_map/reduce_scatter | solution.py:332
  1106.6 489.6 %reduce-scatter.19.cloned.1.call-start = ((), (), s32[]{:S(2)}) async-start(), calls=%async_computation.21 | async-start | bytes 6488064 | tf_op jit(solution)/shard_map/reduce_scatter | solution.py:329
  1118.9 551.5 %reduce-scatter.17.cloned.1.call-start = ((), (), s32[]{:S(2)}) async-start(), calls=%async_computation.19 | async-start | bytes 1179648 | tf_op jit(solution)/shard_map/reduce_scatter | solution.py:328
  1125.7 628.3 %reduce-scatter.15.cloned.1.call-start = ((), (), s32[]{:S(2)}) async-start(), calls=%async_computation.18 | async-start | bytes 3538944 | tf_op jit(solution)/shard_map/reduce_scatter | solution.py:324
  1134.0 282.5 %copy-start = (bf16[128,2048]{1,0:T(8,128)(2,1)S(1)}, bf16[128,2048]{1,0:T(8,128)(2,1)}, u32[]{:S(2)}) copy-start(bf16[128,2048]{1,0:T(8,128)(2,1)} %param.16) | copy-start | bytes 1572868
  1134.0 282.5 %copy-start.22 = (f32[8,1,256]{2,1,0:T(1,128)S(1)}, f32[8,1,256]{2,1,0:T(1,128)}, u32[]{:S(2)}) copy-start(f32[8,1,256]{2,1,0:T(1,128)} %copy-done.21) | copy-start | bytes 24580
  1134.0 282.5 %copy-start.28 = (f32[128]{0:T(128)S(1)}, f32[128]{0:T(128)}, u32[]{:S(2)}) copy-start(f32[128]{0:T(128)} %copy-done.27) | copy-start | bytes 1540
  1134.0 282.5 %copy-start.30 = (f32[128]{0:T(128)S(1)}, f32[128]{0:T(128)}, u32[]{:S(2)}) copy-start(f32[128]{0:T(128)} %copy-done.29) | copy-start | bytes 1540
  1134.0 354.8 %copy-start.6 = (f32[128,2048]{1,0:T(8,128)S(1)}, f32[128,2048]{1,0:T(8,128)}, u32[]{:S(2)}) copy-start(f32[128,2048]{1,0:T(8,128)} %get-tuple-element.532) | copy-start | bytes 3145732
  (37 other events, 180.9 us)
Sparse Core Ops, SparseCore 0:
  10.8 52.2 all-gather.16
  65.3 53.9 all-gather.14
  121.0 52.7 all-gather.12
  204.9 362.4 all-reduce.11
  570.0 59.9 all-gather.18
  632.7 46.4 all-gather.20
  680.9 50.0 all-gather.22
  752.9 183.4 reduce-scatter.10
  941.5 50.7 all-gather.24
  993.8 53.1 all-gather.26
  1049.4 183.4 reduce-scatter.8
  1235.2 181.2 reduce-scatter.12
  1420.8 77.2 reduce-scatter.20
  1502.4 93.7 reduce-scatter.18
  1600.2 70.2 reduce-scatter.16
  1675.2 78.8 reduce-scatter.14
where the time goes:
time: 1770 us; the launch traced here: 1760 us
  waiting for transfers between devices  1170 us (66%)
  blocking collectives  246 us (14%)
  matrix products  154 us (9%)
  other arithmetic  81.1 us (5%)
  local copies, waits for them, and re-layouts  61.2 us (3%)
  loops' own time  32 us (2%)
    psum x1, waiting for transfers between devices, per_device(): lax.psum(jnp.dot(attended, output_full, preferred_element_type=jnp.float3...  320 us
    reduce_scatter x1, waiting for transfers between devices, per_device(): lax.psum_scatter(matmul_nt(gate_up_grad, back_gate_up_flat), 'tensor', sc...  184 us
    reduce_scatter x1, waiting for transfers between devices, per_device(): lax.psum_scatter(matmul_nt(projected_grad, back_heads_flat), 'tensor', sc...  156 us
    reduce_scatter x1, waiting for transfers between devices, per_device(): lax.psum_scatter(grad_gate_up.reshape(D, 2, ffn_local), 'dp', scatter_dim...  98.1 us
    reduce_scatter x1, waiting for transfers between devices, per_device(): lax.psum_scatter(jnp.dot(hidden, down_full, preferred_element_type=jnp.fl...  97.1 us
    unnamed x2, blocking collectives  92.3 us
    reduce_scatter x1, waiting for transfers between devices, per_device(): lax.psum_scatter(grad_heads.reshape(D, 3, width_local), 'dp', scatter_dim...  83.6 us
    reduce_scatter x1, waiting for transfers between devices, per_device(): lax.psum_scatter(grad_output, 'dp', scatter_dimension=1, tiled=True)  74.3 us
  transfers between devices with their start and end apart: 16, of which 12 were waited for; matrix products, arithmetic and copies ran while one was open for 14% of the time, Pallas kernels for 0%

commit v1 on v0

v1 whole, which is shorter than its diff:
```python
import math

import jax
import jax.numpy as jnp
import numpy as np
from jax import lax
from jax.sharding import Mesh, PartitionSpec as P

D = 2048
HD = 64
ROT = 16
WINDOW = 512
QB = 512
LEN = 1024

NORM_EPS = 1e-05
BASE_FREQ = 10000.0
FAR_NEGATIVE = -1e30
BF = jnp.bfloat16
F32 = jnp.float32


def layer_norm_parts(values):
    centre = values - jnp.mean(values, axis=-1, keepdims=True)
    inverse = lax.rsqrt(jnp.mean(centre * centre, axis=-1, keepdims=True) + NORM_EPS)
    return (centre * inverse, inverse)


def norm_back(upstream, normed, inverse, gain):
    scaled = upstream * gain
    inner = (
        scaled
        - jnp.mean(scaled, axis=-1, keepdims=True)
        - normed * jnp.mean(scaled * normed, axis=-1, keepdims=True)
    )
    return (inner * inverse, jnp.sum(upstream * normed, axis=0), jnp.sum(upstream, axis=0))


def doc_starts(seg):
    places = jnp.arange(LEN, dtype=jnp.int32)
    before = jnp.concatenate([jnp.full((1,), -1, jnp.int32), seg[:-1]])
    return lax.cummax(jnp.where(seg != before, places, 0), axis=0)


def rotate(values, places, sign):
    half_rot = ROT // 2
    inverse = jnp.exp(jnp.arange(half_rot, dtype=F32) * (-2.0 * math.log(BASE_FREQ) / ROT))
    angles = places.astype(F32)[..., None] * inverse
    cosine = jnp.cos(angles)[..., None, :]
    sine_part = sign * jnp.sin(angles)[..., None, :]
    first_half = values[..., :half_rot]
    second_half = values[..., half_rot:ROT]
    return jnp.concatenate(
        [
            first_half * cosine - second_half * sine_part,
            second_half * cosine + first_half * sine_part,
            values[..., ROT:],
        ],
        axis=-1,
    )


def nt(left, right):
    return lax.dot_general(left, right, (((1,), (1,)), ((), ())), preferred_element_type=F32)


def tn(left, right):
    return lax.dot_general(left, right, (((0,), (0,)), ((), ())), preferred_element_type=F32)


def mm(left, right):
    return jnp.dot(left, right, preferred_element_type=F32)


def gather_w(w):
    return lax.all_gather(w, ("zhi", "dp"), axis=0, tiled=False)


def gather_b(v):
    return lax.all_gather(v, "b", axis=0, tiled=True)


def scatter_b(v):
    return lax.psum_scatter(v.astype(BF), "b", scatter_dimension=0, tiled=True).astype(F32)


def attention(query, keys, values, allowed):
    scores = jnp.einsum("qhd,khd->hqk", query, keys, preferred_element_type=F32)
    scores = jnp.where(allowed[None], scores, FAR_NEGATIVE)
    maxima = jnp.max(scores, axis=-1, keepdims=True)
    weights = jnp.exp(scores - maxima)
    return weights / jnp.sum(weights, axis=-1, keepdims=True)


def per_device(
    tokens,
    segments,
    first_gain,
    first_shift,
    heads_weight,
    heads_bias,
    output_weight,
    second_gain,
    second_shift,
    gate_up_weight,
    down_weight,
    cotangent,
):
    zhi = lax.axis_index("zhi")
    rows = tokens.shape[0]
    seg = lax.dynamic_index_in_dim(segments, zhi, 0, keepdims=False)
    starts = doc_starts(seg)
    index = jnp.arange(LEN, dtype=jnp.int32)
    places = index - starts
    lowest = jnp.maximum(starts, index - (WINDOW - 1))
    allowed = (index[None, :] <= index[:, None]) & (index[None, :] >= lowest[:, None])

    small = jnp.stack([first_gain, first_shift, second_gain, second_shift]).astype(BF)
    small = lax.all_gather(small, "dp", axis=1, tiled=True).astype(F32)
    gain_one, shift_one, gain_two, shift_two = small[0], small[1], small[2], small[3]
    bias = gather_w(heads_bias.astype(BF).reshape(6, 8)).astype(F32)
    bias = bias.reshape(2, 8, 3, 2, 8).transpose(2, 0, 3, 1, 4).reshape(3, 4, HD)
    w_heads = gather_w(heads_weight.astype(BF)).reshape(2, D, 3, 128)
    w_out = gather_w(output_weight.astype(BF))
    w_gate_up = gather_w(gate_up_weight.astype(BF)).reshape(2, D, 2, 352)
    w_down = gather_w(down_weight.astype(BF))
    w_heads = w_heads.transpose(1, 2, 0, 3).reshape(D, 768)
    w_out = w_out.reshape(2, 8, 128, 256).transpose(0, 2, 1, 3).reshape(256, D)
    w_gate_up = w_gate_up.transpose(1, 2, 0, 3).reshape(D, 1408)
    w_down = w_down.reshape(2, 8, 352, 256).transpose(0, 2, 1, 3).reshape(704, D)

    inputs = tokens.astype(F32)
    normed_one, inverse_one = layer_norm_parts(inputs)
    first_all = gather_b((normed_one * gain_one + shift_one).astype(BF))
    up_all = gather_b(cotangent)
    projected = (mm(first_all, w_heads) + bias.reshape(768)).reshape(LEN, 3, 4, HD)
    query = (rotate(projected[:, 0], places, 1.0) * HD ** (-0.5)).astype(BF)
    keys = rotate(projected[:, 1], places, 1.0).astype(BF)
    values = projected[:, 2].astype(BF)
    probabilities = attention(query, keys, values, allowed)
    prob_low = probabilities.astype(BF)
    attended = (
        jnp.einsum("hqk,khd->qhd", prob_low, values, preferred_element_type=F32)
        .astype(BF)
        .reshape(LEN, 256)
    )
    residual = inputs + scatter_b(mm(attended, w_out))
    normed_two, inverse_two = layer_norm_parts(residual)
    second_all = gather_b((normed_two * gain_two + shift_two).astype(BF))
    gate_up = mm(second_all, w_gate_up)
    gate_pre, up_pre = gate_up[:, :704], gate_up[:, 704:]
    sigmoid_gate = jax.nn.sigmoid(gate_pre)
    silu_gate = gate_pre * sigmoid_gate
    hidden = (silu_gate * up_pre).astype(BF)
    mixed = residual + scatter_b(mm(hidden, w_down))

    hidden_grad = nt(up_all, w_down)
    grad_down = tn(hidden, up_all)
    gate_grad = hidden_grad * up_pre * sigmoid_gate * (1.0 + gate_pre * (1.0 - sigmoid_gate))
    up_grad = hidden_grad * silu_gate
    gate_up_grad = jnp.concatenate([gate_grad, up_grad], axis=1).astype(BF)
    grad_gate_up = tn(second_all, gate_up_grad)
    second_grad = scatter_b(nt(gate_up_grad, w_gate_up))
    residual_part, grad_gain_two, grad_shift_two = norm_back(
        second_grad, normed_two, inverse_two, gain_two
    )
    residual_grad = cotangent.astype(F32) + residual_part
    branch_all = gather_b(residual_grad.astype(BF))
    attended_grad = nt(branch_all, w_out).astype(BF).reshape(LEN, 4, HD)
    grad_output = tn(attended, branch_all)

    prob_grad = jnp.einsum("qhd,khd->hqk", attended_grad, values, preferred_element_type=F32)
    row_inner = jnp.sum(probabilities * prob_grad, axis=-1, keepdims=True)
    score_grad = (probabilities * (prob_grad - row_inner)).astype(BF)
    query_grad = jnp.einsum("hqk,khd->qhd", score_grad, keys, preferred_element_type=F32)
    key_grad = jnp.einsum("hqk,qhd->khd", score_grad, query, preferred_element_type=F32)
    value_grad = jnp.einsum("hqk,qhd->khd", prob_low, attended_grad, preferred_element_type=F32)
    projected_grad = jnp.stack(
        [
            rotate(query_grad * HD ** (-0.5), places, -1.0),
            rotate(key_grad, places, -1.0),
            value_grad,
        ],
        axis=1,
    )
    projected_grad = projected_grad.astype(BF).reshape(LEN, 768)
    grad_bias = jnp.sum(projected_grad.astype(F32), axis=0)
    grad_heads = tn(first_all, projected_grad)
    first_grad = scatter_b(nt(projected_grad, w_heads))
    input_part, grad_gain_one, grad_shift_one = norm_back(
        first_grad, normed_one, inverse_one, gain_one
    )
    grad_tokens = residual_grad + input_part

    def scatter_w(v):
        return lax.psum_scatter(v, ("zhi", "dp"), scatter_dimension=0, tiled=False)

    grad_heads = grad_heads.astype(BF).reshape(8, 256, 3, 2, 128).transpose(3, 0, 1, 2, 4)
    grad_gate_up = grad_gate_up.astype(BF).reshape(8, 256, 2, 2, 352).transpose(3, 0, 1, 2, 4)
    grad_output = grad_output.astype(BF).reshape(2, 128, 8, 256).transpose(0, 2, 1, 3)
    grad_down = grad_down.astype(BF).reshape(2, 352, 8, 256).transpose(0, 2, 1, 3)
    grad_heads = scatter_w(grad_heads.reshape(16, 256, 3, 128)).astype(F32)
    grad_gate_up = scatter_w(grad_gate_up.reshape(16, 256, 2, 352)).astype(F32)
    grad_output = scatter_w(grad_output.reshape(16, 128, 256)).astype(F32)
    grad_down = scatter_w(grad_down.reshape(16, 352, 256)).astype(F32)
    grad_bias = grad_bias.reshape(3, 2, 2, 8, 8).transpose(1, 3, 0, 2, 4).reshape(16, 3, 2, 8)
    grad_bias = scatter_w(grad_bias)
    norms = jnp.stack([grad_gain_one, grad_shift_one, grad_gain_two, grad_shift_two])
    norms = lax.psum_scatter(norms, ("dp", "zhi", "b"), scatter_dimension=1, tiled=True)
    return (
        mixed,
        grad_tokens,
        norms[0],
        norms[1],
        grad_heads,
        grad_bias,
        grad_output,
        norms[2],
        norms[3],
        grad_gate_up,
        grad_down,
    )


T = ("zhi", "b")
ALL = ("dp", "zhi", "b")


def solution(mesh):
    fine = Mesh(np.asarray(mesh.devices).reshape(8, 2, 8), ("dp", "zhi", "b"))
    return jax.shard_map(
        per_device,
        mesh=fine,
        in_specs=(
            P(ALL, None),
            P("dp", None),
            P("dp"),
            P("dp"),
            P("dp", None, T),
            P(None, T, "dp"),
            P(T, "dp"),
            P("dp"),
            P("dp"),
            P("dp", None, T),
            P(T, "dp"),
            P(ALL, None),
        ),
        out_specs=(
            P(ALL, None),
            P(ALL, None),
            P(ALL),
            P(ALL),
            P("dp", None, T),
            P(None, T, "dp"),
            P(T, "dp"),
            P(ALL),
            P(ALL),
            P("dp", None, T),
            P(T, "dp"),
        ),
        check_vma=False,
    )
```

time: 1770 us -> 1890 us (1.068)
  waiting for transfers between devices: 1170 us -> 1400 us
  blocking collectives: 246 us -> 176 us
  local copies, waits for them, and re-layouts: 61.2 us -> 99.9 us
  loops' own time: 32 us -> 0 us
  matrix products: 154 us -> 130 us
    unnamed x16 -> x18, waiting for transfers between devices: 1.61 us -> 638 us
    psum x1 -> x0, waiting for transfers between devices: 320 us -> none  [per_device(): lax.psum(jnp.dot(attended, output_full, preferred_element_type=jnp.float3...]
    reduce_scatter x7 -> x8, waiting for transfers between devices: 699 us -> 458 us  [the longest x4 251 us: scatter_w(): return lax.psum_scatter(v, ('zhi', 'dp'), scatter_dimension=0, tiled=False)]
    all_gather x8, waiting for transfers between devices: 150 us -> 299 us  [the longest x4 235 us: gather_w(): return lax.all_gather(w, ('zhi', 'dp'), axis=0, tiled=False)]
    all_gather x6 -> x2, blocking collectives: 153 us -> 82.4 us  [the longest x1 52 us: gather_w(): return lax.all_gather(w, ('zhi', 'dp'), axis=0, tiled=False)]
    reshape x1 -> x7, local copies, waits for them, and re-layouts: 0.1 us -> 39.1 us  [the longest x1 16.3 us: per_device(): grad_gate_up.astype(BF).reshape(8, 256, 2, 2, 352).transpose(3, 0, 1, 2, 4)]
    transpose x0 -> x8, local copies, waits for them, and re-layouts: none -> 37.2 us  [the longest x1 16 us: per_device(): grad_gate_up.astype(BF).reshape(8, 256, 2, 2, 352).transpose(3, 0, 1, 2, 4)]
    another operation x2 -> x0, loops' own time: 32 us -> none  [the longest x1 18.7 us: per_device(): lax.scan(back_block, (zero_pad, zero_pad), block_ids)]
  transfers between devices with their start and end apart: 16 -> 17, of which waited for: 12 -> 14; matrix products, arithmetic and copies ran while one was open for 14% -> 11% of each run, Pallas kernels for 0% -> 0%
where the time goes in v1:
time: 1890 us; the launch traced here: 1880 us
  waiting for transfers between devices  1400 us (74%)
  blocking collectives  176 us (9%)
  matrix products  130 us (7%)
  local copies, waits for them, and re-layouts  99.9 us (5%)
  other arithmetic  65.7 us (3%)
    unnamed x18, waiting for transfers between devices  638 us
    reduce_scatter x4, waiting for transfers between devices, scatter_w(): return lax.psum_scatter(v, ('zhi', 'dp'), scatter_dimension=0, tiled=False)  251 us
    all_gather x4, waiting for transfers between devices, gather_w(): return lax.all_gather(w, ('zhi', 'dp'), axis=0, tiled=False)  235 us
    reduce_scatter x4, waiting for transfers between devices, scatter_b(): lax.psum_scatter(v.astype(BF), 'b', scatter_dimension=0, tiled=True)  207 us
    unnamed x1, blocking collectives  93.2 us
    all_gather x4, waiting for transfers between devices, gather_b(): return lax.all_gather(v, 'b', axis=0, tiled=True)  64.1 us
    all_gather x1, blocking collectives, gather_w(): return lax.all_gather(w, ('zhi', 'dp'), axis=0, tiled=False)  52 us
  transfers between devices with their start and end apart: 17, of which 14 were waited for; matrix products, arithmetic and copies ran while one was open for 11% of the time, Pallas kernels for 0%

profile of v1, /device:TPU:0, one launch (start us, length us, event | category | flops | bytes accessed | tf_op | source)
XLA Modules:
  0.0 1882.6 jit_solution(15607850332029140423)
XLA Ops:
  13.4 30.3 %all_gather.42 = bf16[4,2048]{1,0:T(4,128)(2,1)S(1)} all-gather(bf16[4,256]{1,0:T(4,128)(2,1)S(1)} %pad_maximum_fusion.7), channel_id=1, replica_groups=mesh['dp'=8,'zhi'=2,'b'=8] {'dp'}, dimensions={1}, use_global_device_ids=true | all-gather | bytes 18432 | tf_op jit(solution)/shard_map/all_gather | solution.py:119
  49.9 52.0 %all_gather.46 = bf16[16,6,8]{2,1,0:T(8,128)(2,1)S(1)} all-gather(bf16[1,6,8]{2,1,0:T(8,128)(2,1)S(1)} %all_gather_reshape.3), channel_id=1, replica_groups=mesh['dp'=8,'zhi'=2,'b'=8] {'zhi','dp'}, dimensions={0}, use_global_device_ids=true | all-gather | bytes 1632 | tf_op jit(solution)/shard_map/all_gather | solution.py:76
  106.0 55.0 %all-gather.21.cloned.1.call-done = bf16[4096,3,128]{2,0,1:T(8,128)(2,1)} async-done(((bf16[256,3,128]{2,0,1:T(8,128)(2,1)}), bf16[4096,3,128]{2,0,1:T(8,128)(2,1)}) %all-gather.21.cloned.1.call-update) | async-done | bytes 3145744 | tf_op jit(solution)/shard_map/all_gather | solution.py:76
  165.9 27.6 %all-gather.13.cloned.1.call-done = bf16[1024,2048]{1,0:T(8,128)(2,1)} async-done(((bf16[128,2048]{1,0:T(8,128)(2,1)}), bf16[1024,2048]{1,0:T(8,128)(2,1)}) %all-gather.13.cloned.1.call-update) | async-done | bytes 4194320 | tf_op jit(solution)/shard_map/all_gather | solution.py:80
  210.5 18.3 fusion.61
  242.6 50.8 %reduce-scatter.12.cloned.1.call-done = bf16[128,2048]{1,0:T(8,128)(2,1)} async-done(((bf16[1024,2048]{1,0:T(8,128)(2,1)}), bf16[128,2048]{1,0:T(8,128)(2,1)}) %reduce-scatter.12.cloned.1.call-update) | async-done | bytes 524304 | tf_op jit(solution)/shard_map/reduce_scatter | solution.py:84
  299.2 74.4 %all-gather.27.cloned.1.call-done = bf16[5632,256]{1,0:T(8,128)(2,1)} async-done(((bf16[352,256]{1,0:T(8,128)(2,1)}), bf16[5632,256]{1,0:T(8,128)(2,1)}) %all-gather.27.cloned.1.call-update) | async-done | bytes 2883600 | tf_op jit(solution)/shard_map/all_gather | solution.py:76
  379.6 105.8 %all-gather.25.cloned.1.call-done = bf16[4096,2,352]{0,2,1:T(8,128)(2,1)} async-done(((bf16[256,2,352]{0,2,1:T(8,128)(2,1)}), bf16[4096,2,352]{0,2,1:T(8,128)(2,1)}) %all-gather.25.cloned.1.call-update) | async-done | bytes 5767184 | tf_op jit(solution)/shard_map/all_gather | solution.py:76
  485.4 10.5 reshape.312
  504.2 13.9 all-gather.15.cloned.1.call-done
  518.0 11.8 fusion.62
  529.9 22.5 %all-gather.17.cloned.1.call-done = bf16[1024,2048]{1,0:T(8,128)(2,1)} async-done(((bf16[128,2048]{1,0:T(8,128)(2,1)}), bf16[1024,2048]{1,0:T(8,128)(2,1)}) %all-gather.17.cloned.1.call-update) | async-done | bytes 4194320 | tf_op jit(solution)/shard_map/all_gather | solution.py:80
  573.2 52.7 %reduce-scatter.16.cloned.1.call-done = bf16[128,2048]{1,0:T(8,128)(2,1)} async-done(((bf16[1024,2048]{1,0:T(8,128)(2,1)}), bf16[128,2048]{1,0:T(8,128)(2,1)}) %reduce-scatter.16.cloned.1.call-update) | async-done | bytes 524304 | tf_op jit(solution)/shard_map/reduce_scatter | solution.py:84
  640.2 11.8 convolution_convert_fusion
  651.9 16.3 reshape.341
  668.2 16.0 copy.128
  693.0 14.3 multiply_reduce_fusion
  709.9 10.7 multiply_convert_fusion
  774.8 105.3 %reduce-scatter.24.cloned.1.call-done = bf16[1,256,2,352]{1,3,2,0:T(8,128)(2,1)} async-done(((bf16[16,256,2,352]{1,3,2,0:T(8,128)(2,1)}), bf16[1,256,2,352]{1,3,2,0:T(8,128)(2,1)}) %reduce-scatter.24.cloned.1.call-update) | async-done | bytes 360464 | tf_op jit(solution)/shard_map/reduce_scatter | solution.py:196
  882.1 93.2 %all-reduce = f32[16,3,2,8]{3,2,1,0:T(2,128)S(1)} all-reduce(f32[16,3,2,8]{3,2,1,0:T(2,128)S(1)} %bitcast.183), channel_id=12, replica_groups=mesh['dp'=8,'zhi'=2,'b'=8] {'zhi','dp'}, use_global_device_ids=true, to_apply=%region_24.25.clone | all-reduce | flops 768 | bytes 6144
  979.7 144.5 %reduce-scatter.20.cloned.1.call-done = bf16[1,256,3,128]{3,1,2,0:T(8,128)(2,1)} async-done(((bf16[16,256,3,128]{3,1,2,0:T(8,128)(2,1)}), bf16[1,256,3,128]{3,1,2,0:T(8,128)(2,1)}) %reduce-scatter.20.cloned.1.call-update) | async-done | bytes 196624 | tf_op jit(solution)/shard_map/reduce_scatter | solution.py:196
  1125.9 51.3 %reduce-scatter.18.cloned.1.call-done = bf16[128,2048]{1,0:T(8,128)(2,1)} async-done(((bf16[1024,2048]{1,0:T(8,128)(2,1)}), bf16[128,2048]{1,0:T(8,128)(2,1)}) %reduce-scatter.18.cloned.1.call-update) | async-done | bytes 524304 | tf_op jit(solution)/shard_map/reduce_scatter | solution.py:84
  1180.3 51.7 %reduce-scatter.14.cloned.1.call-done = bf16[128,2048]{1,0:T(8,128)(2,1)} async-done(((bf16[1024,2048]{1,0:T(8,128)(2,1)}), bf16[128,2048]{1,0:T(8,128)(2,1)}) %reduce-scatter.14.cloned.1.call-update) | async-done | bytes 524304 | tf_op jit(solution)/shard_map/reduce_scatter | solution.py:84
  1235.6 637.0 %reduce-scatter.28.cloned.1.call-done = f32[16,4]{1,0:T(8,128)} async-done(((f32[2048,4]{1,0:T(8,128)}), f32[16,4]{1,0:T(8,128)}) %reduce-scatter.28.cloned.1.call-update) | async-done | bytes 272
  (260 shorter events, 190.0 us)
Async XLA Ops:
  7.2 96.7 %all-gather.23.cloned.1.call-start = ((), (), s32[]{:S(2)}) async-start(), calls=%async_computation.22 | async-start | bytes 1114112 | tf_op jit(solution)/shard_map/all_gather | solution.py:76
  8.8 152.2 %all-gather.21.cloned.1.call-start = ((), (), s32[]{:S(2)}) async-start(), calls=%async_computation.21 | async-start | bytes 3342336 | tf_op jit(solution)/shard_map/all_gather | solution.py:76
  10.6 183.0 %all-gather.13.cloned.1.call-start = ((), (), s32[]{:S(2)}) async-start(), calls=%async_computation.9 | async-start | bytes 4718592 | tf_op jit(solution)/shard_map/all_gather | solution.py:80
  48.6 244.8 %reduce-scatter.12.cloned.1.call-start = ((), (), s32[]{:S(2)}) async-start(), calls=%async_computation.10 | async-start | bytes 4718592 | tf_op jit(solution)/shard_map/reduce_scatter | solution.py:84
  228.8 464.1 %copy-start.32 = (f32[4,1024]{1,0:T(4,128)}, f32[4,1024]{1,0:T(4,128)S(1)}, u32[]{:S(2)}) copy-start(f32[4,1024]{1,0:T(4,128)S(1)} %get-tuple-element.53) | copy-start | bytes 49156
  240.6 133.0 %all-gather.27.cloned.1.call-start = ((), (), s32[]{:S(2)}) async-start(), calls=%async_computation.24 | async-start | bytes 3063808 | tf_op jit(solution)/shard_map/all_gather | solution.py:76
  241.4 244.0 %all-gather.25.cloned.1.call-start = ((), (), s32[]{:S(2)}) async-start(), calls=%async_computation.23 | async-start | bytes 6127616 | tf_op jit(solution)/shard_map/all_gather | solution.py:76
  242.6 275.5 %all-gather.15.cloned.1.call-start = ((), (), s32[]{:S(2)}) async-start(), calls=%async_computation.11 | async-start | bytes 4718592 | tf_op jit(solution)/shard_map/all_gather | solution.py:80
  298.2 254.2 %all-gather.17.cloned.1.call-start = ((), (), s32[]{:S(2)}) async-start(), calls=%async_computation.13 | async-start | bytes 4718592 | tf_op jit(solution)/shard_map/all_gather | solution.py:80
  299.0 326.9 %reduce-scatter.16.cloned.1.call-start = ((), (), s32[]{:S(2)}) async-start(), calls=%async_computation.14 | async-start | bytes 4718592 | tf_op jit(solution)/shard_map/reduce_scatter | solution.py:84
  573.1 111.1 %all-gather.19.cloned.1.call-start = ((), (), s32[]{:S(2)}) async-start(), calls=%async_computation.15 | async-start | bytes 4718592 | tf_op jit(solution)/shard_map/all_gather | solution.py:80
  630.7 142.5 %reduce-scatter.26.cloned.1.call-start = ((), (), s32[]{:S(2)}) async-start(), calls=%async_computation.20 | async-start | bytes 3063808 | tf_op jit(solution)/shard_map/reduce_scatter | solution.py:196
  640.1 240.0 %reduce-scatter.24.cloned.1.call-start = ((), (), s32[]{:S(2)}) async-start(), calls=%async_computation.19 | async-start | bytes 6127616 | tf_op jit(solution)/shard_map/reduce_scatter | solution.py:196
  684.2 294.0 %reduce-scatter.22.cloned.1.call-start = ((), (), s32[]{:S(2)}) async-start(), calls=%async_computation.18 | async-start | bytes 1114112 | tf_op jit(solution)/shard_map/reduce_scatter | solution.py:196
  728.9 395.3 %reduce-scatter.20.cloned.1.call-start = ((), (), s32[]{:S(2)}) async-start(), calls=%async_computation.17 | async-start | bytes 3342336 | tf_op jit(solution)/shard_map/reduce_scatter | solution.py:196
  755.9 421.3 %reduce-scatter.18.cloned.1.call-start = ((), (), s32[]{:S(2)}) async-start(), calls=%async_computation.16 | async-start | bytes 4718592 | tf_op jit(solution)/shard_map/reduce_scatter | solution.py:84
  764.2 467.8 %reduce-scatter.14.cloned.1.call-start = ((), (), s32[]{:S(2)}) async-start(), calls=%async_computation.12 | async-start | bytes 4718592 | tf_op jit(solution)/shard_map/reduce_scatter | solution.py:84
  771.9 460.1 %copy-start.8 = (bf16[128,2048]{1,0:T(8,128)(2,1)S(1)}, bf16[128,2048]{1,0:T(8,128)(2,1)}, u32[]{:S(2)}) copy-start(bf16[128,2048]{1,0:T(8,128)(2,1)} %reduce-scatter.16.cloned.1.call-done) | copy-start | bytes 1572868
  771.9 460.1 %copy-start.36 = (f32[128]{0:T(128)S(1)}, f32[128]{0:T(128)}, u32[]{:S(2)}) copy-start(f32[128]{0:T(128)} %copy-done.35) | copy-start | bytes 1540
  771.9 460.1 %copy-start.40 = (f32[128]{0:T(128)S(1)}, f32[128]{0:T(128)}, u32[]{:S(2)}) copy-start(f32[128]{0:T(128)} %copy-done.39) | copy-start | bytes 1540
  771.9 460.1 %copy-start.44 = (f32[128]{0:T(128)S(1)}, f32[128]{0:T(128)}, u32[]{:S(2)}) copy-start(f32[128]{0:T(128)} %copy-done.43) | copy-start | bytes 1540
  772.0 460.0 %copy-start.46 = (f32[128]{0:T(128)S(1)}, f32[128]{0:T(128)}, u32[]{:S(2)}) copy-start(f32[128]{0:T(128)} %copy-done.45) | copy-start | bytes 1540
  772.0 1100.6 %reduce-scatter.28.cloned.1.call-start = ((), (), s32[]{:S(2)}) async-start(), calls=%async_computation.25 | async-start | bytes 1056768
  1124.2 751.6 %copy-start.1 = (s32[2,1024]{1,0:T(2,128)S(1)}, s32[2,1024]{1,0:T(2,128)}, u32[]{:S(2)}) copy-start(s32[2,1024]{1,0:T(2,128)} %param.13) | copy-start | bytes 24580
  (52 other events, 3278.4 us)
Sparse Core Ops, SparseCore 0:
  11.8 68.6 all-gather.22
  84.3 76.7 all-gather.20
  163.3 30.2 all-gather.12
  240.8 52.6 reduce-scatter.11
  296.5 77.1 all-gather.26
  377.1 108.3 all-gather.24
  487.7 30.2 all-gather.14
  519.7 32.6 all-gather.16
  573.3 52.6 reduce-scatter.15
  630.8 32.3 all-gather.18
  665.6 105.4 reduce-scatter.25
  773.4 106.6 reduce-scatter.23
  883.0 95.1 reduce-scatter.21
  984.4 139.7 reduce-scatter.19
  1126.6 50.6 reduce-scatter.17
  1179.6 52.3 reduce-scatter.13
  1234.3 638.2 reduce-scatter.27

commit v2 on v1

v2 whole, which is shorter than its diff:
```python
import functools
import math

import jax
import jax.numpy as jnp
from jax import lax
from jax.experimental import pallas as pl
from jax.experimental.pallas import tpu as pltpu
from jax.sharding import PartitionSpec as P

D = 2048
HD = 64
ROT = 16
WINDOW = 512
LEN = 1024
OWN = 128
HALF = OWN // 2
CHIP = 2 * OWN
UNITS = 352
PAD = 384
QB = 256

NORM_EPS = 1e-05
BASE_FREQ = 10000.0
FAR_NEGATIVE = -1e30
BF = jnp.bfloat16
F32 = jnp.float32
MESH = pl.DeviceIdType.MESH
VMEM_LIMIT = 60 * 2**20
DMA = pltpu.SemaphoreType.DMA


def spot(z, x, c):
    return (z % 2) * 4 + x * 2 + c


class Near:
    def __init__(self):
        t = lax.axis_index("tensor")
        z, x, c = t // 4, (t // 2) % 2, t % 2
        oz = (z // 2) * 2 + (z + 1) % 2
        ox, oc = 1 - x, 1 - c
        self.c, self.oc = c, oc
        self.me = spot(z, x, c)
        self.dev = {
            "x": {"tensor": z * 4 + ox * 2 + c},
            "z": {"tensor": oz * 4 + x * 2 + c},
            "s": {"tensor": z * 4 + x * 2 + oc},
        }
        self.same = {"o": spot(z, x, c), "x": spot(z, ox, c), "z": spot(oz, x, c), "d": spot(oz, ox, c)}
        self.other = {
            "o": spot(z, x, oc),
            "x": spot(z, ox, oc),
            "z": spot(oz, x, oc),
            "d": spot(oz, ox, oc),
        }
        self.chip = {"o": (z % 2) * 2 + x, "x": (z % 2) * 2 + ox, "z": (oz % 2) * 2 + x, "d": (oz % 2) * 2 + ox}


def remote(src, dst, send, recv, device):
    return pltpu.make_async_remote_copy(
        src_ref=src, dst_ref=dst, send_sem=send, recv_sem=recv, device_id=device, device_id_type=MESH
    )


def greet(devices):
    barrier = pltpu.get_barrier_semaphore()
    for device in devices:
        pl.semaphore_signal(barrier, inc=1, device_id=device, device_id_type=MESH)
    pl.semaphore_wait(barrier, len(devices))


def block_rows(block, half=None):
    if half is None:
        return pl.ds(pl.multiple_of(block * OWN, OWN), OWN)
    return pl.ds(pl.multiple_of(block * OWN + half * HALF, HALF), HALF)


def chip_rows(chip):
    return pl.ds(pl.multiple_of(chip * CHIP, CHIP), CHIP)


class Gather:
    COPIES = 13

    def __init__(self, near, buf, send, recv):
        self.near, self.buf, self.send, self.recv = near, buf, send, recv
        self.sent = []

    def copy(self, index, block, half, to):
        view = self.buf.at[block_rows(block, half)]
        return remote(view, view, self.send.at[index], self.recv.at[index], self.near.dev[to])

    def go(self, index, block, half, to):
        copy = self.copy(index, block, half, to)
        copy.start()
        self.sent.append(copy)

    def take(self, index, block, half, to="s"):
        self.copy(index, block, half, to).wait_recv()

    def start(self):
        me = self.near.me
        self.go(0, me, 0, "z")
        self.go(1, me, 1, "x")
        self.go(4, me, None, "s")
        self.go(2, me, 0, "x")
        self.go(3, me, 1, "z")

    def first(self):
        same = self.near.same
        self.take(0, same["z"], 0)
        self.go(5, same["z"], 0, "x")
        self.go(7, same["z"], 0, "s")
        self.take(1, same["x"], 1)
        self.go(6, same["x"], 1, "z")
        self.go(8, same["x"], 1, "s")

    def second(self):
        same = self.near.same
        self.take(2, same["x"], 0)
        self.go(9, same["x"], 0, "s")
        self.take(3, same["z"], 1)
        self.go(10, same["z"], 1, "s")

    def third(self):
        same = self.near.same
        self.take(5, same["d"], 0)
        self.go(11, same["d"], 0, "s")
        self.take(6, same["d"], 1)
        self.go(12, same["d"], 1, "s")

    def own_chip(self):
        self.take(4, self.near.other["o"], None)

    def x_chip(self):
        self.take(8, self.near.other["x"], 1)
        self.take(9, self.near.other["x"], 0)

    def z_chip(self):
        self.take(7, self.near.other["z"], 0)
        self.take(10, self.near.other["z"], 1)

    def d_chip(self):
        self.take(11, self.near.other["d"], 0)
        self.take(12, self.near.other["d"], 1)

    def finish(self):
        for copy in self.sent:
            copy.wait_send()

    def run(self, use):
        self.own_chip()
        use("o")
        self.first()
        self.second()
        self.x_chip()
        use("x")
        self.third()
        self.z_chip()
        use("z")
        self.d_chip()
        use("d")


class Scatter:
    COPIES = 10

    @staticmethod
    def scratch(width=D):
        return [
            pltpu.VMEM((CHIP, width), F32),
            pltpu.VMEM((4, OWN, width), F32),
            pltpu.VMEM((4, OWN, width), BF),
            pltpu.VMEM((4, OWN, width), BF),
            pltpu.VMEM((OWN, width), BF),
            pltpu.VMEM((4, HALF, width), BF),
            pltpu.VMEM((2, HALF, width), BF),
            pltpu.VMEM((4, HALF, width), BF),
            DMA((Scatter.COPIES,)),
            DMA((Scatter.COPIES,)),
        ]

    KEYS = ("d", "z", "x", "o")

    def __init__(self, near, refs):
        self.near = near
        (
            self.part,
            self.mine,
            self.core_out,
            self.core_in,
            self.far_out,
            self.out,
            self.through,
            self.last,
            self.send,
            self.recv,
        ) = refs
        self.sent = []

    def copy(self, index, src, dst, to):
        return remote(src, dst, self.send.at[index], self.recv.at[index], self.near.dev[to])

    def go(self, index, src, dst, to):
        copy = self.copy(index, src, dst, to)
        copy.start()
        self.sent.append(copy)

    def take(self, index, dst, to="s"):
        self.copy(index, dst, dst, to).wait_recv()

    def produce(self, key, make):
        i = self.KEYS.index(key)
        make(self.near.chip[key])
        self.core_out[i] = self.part[block_rows(self.near.oc), :].astype(BF)
        self.go(i, self.core_out.at[i], self.core_in.at[i], "s")
        self.mine[i] = self.part[block_rows(self.near.c), :]

    def join(self, key):
        i = self.KEYS.index(key)
        self.take(i, self.core_in.at[i])

    def summed(self, key, half):
        i = self.KEYS.index(key)
        rows = slice(half * HALF, (half + 1) * HALF)
        return self.mine[i, rows, :] + self.core_in[i, rows, :].astype(F32)

    def far(self):
        self.join("d")
        self.far_out[:HALF, :] = self.summed("d", 0).astype(BF)
        self.go(4, self.far_out.at[pl.ds(0, HALF)], self.through.at[0], "z")
        self.far_out[HALF:, :] = self.summed("d", 1).astype(BF)
        self.go(5, self.far_out.at[pl.ds(HALF, HALF)], self.through.at[1], "x")

    def z_direct(self):
        self.join("z")
        self.out[0] = self.summed("z", 0).astype(BF)
        self.go(6, self.out.at[0], self.last.at[0], "z")

    def x_direct(self):
        self.join("x")
        self.out[1] = self.summed("x", 1).astype(BF)
        self.go(7, self.out.at[1], self.last.at[1], "x")

    def relays(self):
        self.take(4, self.through.at[0])
        self.out[2] = (self.summed("x", 0) + self.through[0].astype(F32)).astype(BF)
        self.go(8, self.out.at[2], self.last.at[2], "x")
        self.take(5, self.through.at[1])
        self.out[3] = (self.summed("z", 1) + self.through[1].astype(F32)).astype(BF)
        self.go(9, self.out.at[3], self.last.at[3], "z")

    def result(self):
        self.join("o")
        for index in range(4):
            self.take(6 + index, self.last.at[index])
        first = self.summed("o", 0) + self.last[0].astype(F32) + self.last[2].astype(F32)
        second = self.summed("o", 1) + self.last[1].astype(F32) + self.last[3].astype(F32)
        for copy in self.sent:
            copy.wait_send()
        self.sent = []
        return first, second

    def run(self, make):
        self.produce("d", make)
        self.produce("z", make)
        self.far()
        self.produce("x", make)
        self.z_direct()
        self.produce("o", make)
        self.x_direct()
        self.relays()
        return self.result()


def dot(left, right):
    return jnp.dot(left, right, preferred_element_type=F32)


def dot_nt(left, right):
    return lax.dot_general(left, right, (((1,), (1,)), ((), ())), preferred_element_type=F32)


def dot_tn(left, right):
    return lax.dot_general(left, right, (((0,), (0,)), ((), ())), preferred_element_type=F32)


def layer_norm_parts(values):
    centre = values - jnp.mean(values, axis=-1, keepdims=True)
    inverse = lax.rsqrt(jnp.mean(centre * centre, axis=-1, keepdims=True) + NORM_EPS)
    return (centre * inverse, inverse)


def norm_back(upstream, normed, inverse, gain):
    scaled = upstream * gain
    inner = (
        scaled
        - jnp.mean(scaled, axis=-1, keepdims=True)
        - normed * jnp.mean(scaled * normed, axis=-1, keepdims=True)
    )
    return (
        inner * inverse,
        jnp.sum(upstream * normed, axis=0, keepdims=True),
        jnp.sum(upstream, axis=0, keepdims=True),
    )


def params(collective=None):
    if collective is None:
        return pltpu.CompilerParams(vmem_limit_bytes=VMEM_LIMIT)
    return pltpu.CompilerParams(
        collective_id=collective, has_side_effects=True, vmem_limit_bytes=VMEM_LIMIT
    )


def cost(flops, moved):
    return pl.CostEstimate(flops=flops, bytes_accessed=moved, transcendentals=0)


IN_VMEM = pl.BlockSpec(memory_space=pltpu.VMEM)
ANYWHERE = pl.BlockSpec(memory_space=pl.ANY)


def shape(dims, dtype):
    return jax.ShapeDtypeStruct(dims, dtype)


def copy_all(pairs, sems):
    copies = [pltpu.make_async_copy(src, dst, sems.at[i]) for i, (src, dst) in enumerate(pairs)]
    for copy in copies:
        copy.start()
    return copies


def dp_of(k, h):
    dp = lax.axis_index("dp")
    return ((dp // 4 + h) % 2) * 4 + (dp % 4 - k + 4) % 4


def weight_pairs(blocks, buf):
    pairs = []
    if len(blocks) == 4:
        for k in range(4):
            for h in range(2):
                for s in range(2):
                    row = pl.ds(pl.multiple_of(dp_of(k, h) * 256, 256), 256)
                    pairs.append((blocks[k].at[h * 2 + s], buf.at[s, row]))
    else:
        for k in range(4):
            for h in range(2):
                row = pl.ds(pl.multiple_of(dp_of(k, h) * 256, 256), 256)
                pairs.append((blocks[k].at[h], buf.at[0, row]))
                pairs.append((blocks[4].at[k * 2 + h], buf.at[1, row]))
    return pairs


def open_kernel(
    tok, cot, small, head, first_out, cot_out, gains_out, head_out,
    fa, ca, gbuf, ga_send, ga_recv, gc_send, gc_recv, sm_send, sm_recv, hd_send, hd_recv, out_sem,
):
    near = Near()
    t, dp = lax.axis_index("tensor"), lax.axis_index("dp")
    h, y = dp // 4, dp % 4
    over = {"dp": (1 - h) * 4 + y}
    ring = [{"dp": h * 4 + (y + k) % 4} for k in (1, 2, 3)]
    partner = {"tensor": (3 - t // 4) * 4 + t % 4}
    greet([near.dev["x"], near.dev["z"], near.dev["s"], over, partner] + ring)

    small_sent = []

    def send_small(index, slot_from, slot_to, device, src=None):
        copy = remote(
            gbuf.at[slot_from] if src is None else src,
            gbuf.at[slot_to],
            sm_send.at[index],
            sm_recv.at[index],
            device,
        )
        copy.start()
        small_sent.append(copy)

    def take_small(index, slot):
        remote(gbuf.at[slot], gbuf.at[slot], sm_send.at[index], sm_recv.at[index], over).wait_recv()

    send_small(0, 0, 1, over, small)
    for k in (1, 2, 3):
        send_small(k, 0, k * 2, ring[k - 1], small)

    head_sent = []

    def send_head(index, slot_from, slot_to, device, src=None):
        copy = remote(
            head_out.at[slot_from] if src is None else src,
            head_out.at[slot_to],
            hd_send.at[index],
            hd_recv.at[index],
            device,
        )
        copy.start()
        head_sent.append(copy)

    def take_head(index, slot):
        remote(head_out.at[slot], head_out.at[slot], hd_send.at[index], hd_recv.at[index], over).wait_recv()

    send_head(0, 0, 1, partner, head)
    send_head(1, 0, 2, over, head)
    for k in (1, 2, 3):
        send_head(3 + (k - 1) * 4, 0, k * 4, ring[k - 1], head)

    ca[block_rows(near.me), :] = cot[...]
    cots = Gather(near, ca, gc_send, gc_recv)
    cots.start()
    gbuf[0] = small[...]
    own_head = pltpu.make_async_copy(head, head_out.at[0], out_sem.at[8])
    own_head.start()

    normed, _ = layer_norm_parts(tok[...].astype(F32))
    take_small(0, 1)
    for k in (1, 2, 3):
        send_small(3 + k, 1, k * 2 + 1, ring[k - 1])
    for k in (1, 2, 3):
        take_small(k, k * 2)
    for k in (1, 2, 3):
        take_small(3 + k, k * 2 + 1)
    for d in range(8):
        slot = ((y - d % 4 + 4) % 4) * 2 + (h + d // 4) % 2
        gains_out[:, d * 256 : (d + 1) * 256] = gbuf[slot]
    first = normed * gains_out[0:1, :] + gains_out[1:2, :]
    fa[block_rows(near.me), :] = first.astype(BF)
    firsts = Gather(near, fa, ga_send, ga_recv)
    firsts.start()

    take_head(0, 1)
    send_head(2, 1, 3, over)
    for k in (1, 2, 3):
        send_head(4 + (k - 1) * 4, 1, k * 4 + 1, ring[k - 1])
    take_head(1, 2)
    for k in (1, 2, 3):
        send_head(5 + (k - 1) * 4, 2, k * 4 + 2, ring[k - 1])

    cots.first()
    cots.second()
    take_head(2, 3)
    for k in (1, 2, 3):
        send_head(6 + (k - 1) * 4, 3, k * 4 + 3, ring[k - 1])
    cots.third()
    firsts.first()
    firsts.second()
    firsts.third()
    copies = []

    def out(index, buf, target, chip):
        rows = chip_rows(chip)
        copy = pltpu.make_async_copy(buf.at[rows], target.at[rows], out_sem.at[index])
        copy.start()
        copies.append(copy)

    for i, (gather, buf, target) in enumerate(((cots, ca, cot_out), (firsts, fa, first_out))):
        gather.own_chip()
        out(i * 4, buf, target, near.chip["o"])
        gather.x_chip()
        out(i * 4 + 1, buf, target, near.chip["x"])
        gather.z_chip()
        out(i * 4 + 2, buf, target, near.chip["z"])
        gather.d_chip()
        out(i * 4 + 3, buf, target, near.chip["d"])
    for k in (1, 2, 3):
        for j in range(4):
            take_head(3 + (k - 1) * 4 + j, k * 4 + j)
    cots.finish()
    firsts.finish()
    for copy in small_sent + head_sent:
        copy.wait_send()
    own_head.wait()
    for copy in copies:
        copy.wait()


def open_call(tokens, cotangent, small, head):
    return pl.pallas_call(
        open_kernel,
        out_shape=(
            shape((LEN, D), BF),
            shape((LEN, D), BF),
            shape((8, D), F32),
            shape((16,) + head.shape, BF),
        ),
        in_specs=[IN_VMEM, IN_VMEM, IN_VMEM, ANYWHERE],
        out_specs=(ANYWHERE, ANYWHERE, IN_VMEM, ANYWHERE),
        scratch_shapes=[
            pltpu.VMEM((LEN, D), BF),
            pltpu.VMEM((LEN, D), BF),
            pltpu.VMEM((8, 8, 256), F32),
            DMA((Gather.COPIES,)),
            DMA((Gather.COPIES,)),
            DMA((Gather.COPIES,)),
            DMA((Gather.COPIES,)),
            DMA((7,)),
            DMA((7,)),
            DMA((15,)),
            DMA((15,)),
            DMA((9,)),
        ],
        compiler_params=params(1),
        cost_estimate=cost(10**9, 60 * 2**20),
        name="open",
    )(tokens, cotangent, small, head)


def roll_rotate(values, cos, sin_up, sin_down):
    return (
        values * cos + pltpu.roll(values, 128 - ROT // 2, 1) * sin_up + pltpu.roll(values, ROT // 2, 1) * sin_down
    )


def window(block):
    start = max(0, block * QB - WINDOW)
    return start, (block + 1) * QB


def mask_bias(lowest, start, stop, block):
    keys = lax.broadcasted_iota(jnp.int32, (stop - start, QB), 0) + start
    queries = lax.broadcasted_iota(jnp.int32, (stop - start, QB), 1) + block * QB
    return jnp.where((keys <= queries) & (keys >= lowest), 0.0, FAR_NEGATIVE)


def head_lanes(rows, head):
    lanes = lax.broadcasted_iota(jnp.int32, (rows, 128), 1)
    return (lanes >= HD) if head else (lanes < HD)


def attend_kernel(
    first, head, cos, sin_up, sin_down, lowest,
    query, keys, values, attended, log_sum,
    wv, extra, vt, w_sem,
):
    copies = []
    for k in range(4):
        for h in range(2):
            for s in range(2):
                slot, dp = k * 4 + h * 2 + s, dp_of(k, h)
                row = pl.ds(pl.multiple_of(dp * 256, 256), 256)
                tail = pl.ds((k * 2 + h) * 16, 16)
                copies.append(
                    pltpu.make_async_copy(head.at[slot, pl.ds(0, 256)], wv.at[s, row], w_sem.at[2 * slot])
                )
                copies.append(
                    pltpu.make_async_copy(head.at[slot, pl.ds(256, 16)], extra.at[s, tail], w_sem.at[2 * slot + 1])
                )
    for copy in copies:
        copy.start()
    for copy in copies:
        copy.wait()
    bias = [jnp.sum(extra[s].astype(F32), axis=0, keepdims=True) for s in range(2)]

    @pl.loop(0, LEN // CHIP)
    def _(step):
        rows = chip_rows(step)
        c, up, down = cos[rows, :], sin_up[rows, :], sin_down[rows, :]
        for s in range(2):
            lanes = slice(s * 128, (s + 1) * 128)
            made = dot(first[rows, :], wv[s]) + bias[s]
            query[rows, lanes] = (roll_rotate(made[:, :128], c, up, down) * HD ** (-0.5)).astype(BF)
            keys[rows, lanes] = roll_rotate(made[:, 128:256], c, up, down).astype(BF)
            values[rows, lanes] = made[:, 256:].astype(BF)
            vt[s, :, rows] = made[:, 256:].T.astype(BF)

    for block in range(LEN // QB):
        start, stop = window(block)
        rows = slice(block * QB, (block + 1) * QB)
        bias_t = mask_bias(lowest[:, rows], start, stop, block)
        for s in range(2):
            lanes = slice(s * 128, (s + 1) * 128)
            q, k = query[rows, lanes], keys[start:stop, lanes]
            v_t = vt[s, :, start:stop]
            halves = []
            for head_id in range(2):
                q_one = jnp.where(head_lanes(QB, head_id), q, jnp.zeros_like(q))
                scores = dot_nt(k, q_one) + bias_t
                top = jnp.max(scores, axis=0, keepdims=True)
                weights = jnp.exp(scores - top)
                total = jnp.sum(weights, axis=0, keepdims=True)
                made = dot(v_t, weights.astype(BF))
                halves.append(made[head_id * HD : (head_id + 1) * HD] * (1.0 / total))
                log_sum[s * 2 + head_id : s * 2 + head_id + 1, rows] = top + jnp.log(total)
            attended[rows, lanes] = jnp.concatenate(halves, axis=0).T.astype(BF)


def attend_call(first_all, head, cos, sin_up, sin_down, lowest):
    narrow = shape((LEN, 256), BF)
    return pl.pallas_call(
        attend_kernel,
        out_shape=(narrow, narrow, narrow, narrow, shape((8, LEN), F32)),
        in_specs=[IN_VMEM, ANYWHERE] + [IN_VMEM] * 4,
        out_specs=(IN_VMEM,) * 5,
        scratch_shapes=[
            pltpu.VMEM((2, D, 384), BF),
            pltpu.VMEM((2, 128, 384), BF),
            pltpu.VMEM((2, 128, LEN), BF),
            DMA((32,)),
        ],
        compiler_params=params(),
        cost_estimate=cost(5 * 10**9, 12 * 2**20),
        name="attend",
    )(first_all, head, cos, sin_up, sin_down, lowest)


def silu_parts(gate, up, grad):
    sig = 1.0 / (1.0 + jnp.exp(-gate))
    silu = gate * sig
    return silu * up, grad * up * sig * (1.0 + gate * (1.0 - sig)), grad * silu


def middle_kernel(
    attended, tok, gains, cot_all, *rest,
):
    wo_in, wg_in, wd_in = rest[0:5], rest[5:9], rest[9:14]
    residual, second_out, hidden_out, grads_out = rest[14:18]
    wo, wg, wd, cots, hg, second, hidden, grads = rest[18:26]
    scatter_refs, (ga_send, ga_recv, w_sem, o_sem) = rest[26:36], rest[36:40]
    near = Near()
    out_copies = copy_all(weight_pairs(wo_in, wo), w_sem.at[pl.ds(0, 16)])
    cot_copy = copy_all([(cot_all, cots)], w_sem.at[pl.ds(48, 1)])
    down_copies = copy_all(weight_pairs(wd_in, wd), w_sem.at[pl.ds(16, 16)])
    gate_copies = copy_all(weight_pairs(wg_in, wg), w_sem.at[pl.ds(32, 16)])
    greet([near.dev["x"], near.dev["z"], near.dev["s"]])
    for copy in out_copies:
        copy.wait()
    scatter = Scatter(near, scatter_refs)

    def make(chip):
        rows = chip_rows(chip)
        scatter.part[...] = dot_nt(attended[rows, :128], wo[0]) + dot_nt(attended[rows, 128:], wo[1])

    scatter.produce("d", make)
    scatter.produce("z", make)
    scatter.far()
    scatter.produce("x", make)
    scatter.z_direct()
    scatter.produce("o", make)
    scatter.x_direct()
    for copy in cot_copy + down_copies:
        copy.wait()
    for chip in range(2):
        for s in range(2):
            hg[s, chip_rows(chip), :] = dot(cots[chip_rows(chip), :], wd[s])
    scatter.relays()
    for chip in range(2, 4):
        for s in range(2):
            hg[s, chip_rows(chip), :] = dot(cots[chip_rows(chip), :], wd[s])
    for copy in gate_copies:
        copy.wait()
    first, second_half = scatter.result()
    residual[:HALF, :] = tok[:HALF, :].astype(F32) + first
    residual[HALF:, :] = tok[HALF:, :].astype(F32) + second_half
    normed, _ = layer_norm_parts(residual[...])
    second[block_rows(near.me), :] = (normed * gains[2:3, :] + gains[3:4, :]).astype(BF)
    gather = Gather(near, second, ga_send, ga_recv)
    gather.start()
    copies = []

    def use(key):
        chip = near.chip[key]
        rows = chip_rows(chip)
        for s in range(2):
            made = dot(second[rows, :], wg[s])
            h, g, u = silu_parts(made[:, :PAD], made[:, PAD:], hg[s, rows, :])
            hidden[rows, s * PAD : (s + 1) * PAD] = h.astype(BF)
            grads[rows, s * 2 * PAD : s * 2 * PAD + PAD] = g.astype(BF)
            grads[rows, s * 2 * PAD + PAD : (s + 1) * 2 * PAD] = u.astype(BF)
        i = "oxzd".index(key) * 3
        copies.extend(
            copy_all(
                [
                    (second.at[rows], second_out.at[rows]),
                    (hidden.at[rows], hidden_out.at[rows]),
                    (grads.at[rows], grads_out.at[rows]),
                ],
                o_sem.at[pl.ds(i, 3)],
            )
        )

    gather.run(use)
    gather.finish()
    for copy in copies:
        copy.wait()


def middle_call(attended, tokens, gains, cot_all, wo, wg, wd):
    return pl.pallas_call(
        middle_kernel,
        out_shape=(
            shape((OWN, D), F32),
            shape((LEN, D), BF),
            shape((LEN, 2 * PAD), BF),
            shape((LEN, 4 * PAD), BF),
        ),
        in_specs=[IN_VMEM, IN_VMEM, IN_VMEM] + [ANYWHERE] * 15,
        out_specs=(IN_VMEM, ANYWHERE, ANYWHERE, ANYWHERE),
        scratch_shapes=[
            pltpu.VMEM((2, D, 128), BF),
            pltpu.VMEM((2, D, 2 * PAD), BF),
            pltpu.VMEM((2, D, PAD), BF),
            pltpu.VMEM((LEN, D), BF),
            pltpu.VMEM((2, LEN, PAD), F32),
            pltpu.VMEM((LEN, D), BF),
            pltpu.VMEM((LEN, 2 * PAD), BF),
            pltpu.VMEM((LEN, 4 * PAD), BF),
            *Scatter.scratch(),
            DMA((Gather.COPIES,)),
            DMA((Gather.COPIES,)),
            DMA((49,)),
            DMA((12,)),
        ],
        compiler_params=params(2),
        cost_estimate=cost(20 * 10**9, 60 * 2**20),
        name="middle",
    )(attended, tokens, gains, cot_all, *wo, *wg, *wd)


def back_kernel(grads, residual, cot, gains, *rest):
    wo_in, wg_in = rest[0:5], rest[5:9]
    residual_grad, branch_out, attended_grad, norm_sums = rest[9:13]
    wo, wg, branch = rest[13:16]
    scatter_refs, (ga_send, ga_recv, w_sem, o_sem) = rest[16:26], rest[26:30]
    near = Near()
    gate_copies = copy_all(weight_pairs(wg_in, wg), w_sem.at[pl.ds(0, 16)])
    out_copies = copy_all(weight_pairs(wo_in, wo), w_sem.at[pl.ds(16, 16)])
    greet([near.dev["x"], near.dev["z"], near.dev["s"]])
    for copy in gate_copies:
        copy.wait()
    scatter = Scatter(near, scatter_refs)

    def make(chip):
        rows = chip_rows(chip)
        scatter.part[...] = dot_nt(grads[rows, : 2 * PAD], wg[0]) + dot_nt(grads[rows, 2 * PAD :], wg[1])

    first, second_half = scatter.run(make)
    normed, inverse = layer_norm_parts(residual[...])
    upstream = jnp.concatenate([first, second_half], axis=0)
    part, gain_sum, shift_sum = norm_back(upstream, normed, inverse, gains[2:3, :])
    made = cot[...].astype(F32) + part
    residual_grad[...] = made
    norm_sums[0:1, :] = gain_sum
    norm_sums[1:2, :] = shift_sum
    branch[block_rows(near.me), :] = made.astype(BF)
    gather = Gather(near, branch, ga_send, ga_recv)
    gather.start()
    for copy in out_copies:
        copy.wait()
    copies = []

    def use(key):
        rows = chip_rows(near.chip[key])
        for s in range(2):
            attended_grad[rows, s * 128 : (s + 1) * 128] = dot(branch[rows, :], wo[s]).astype(BF)
        i = "oxzd".index(key)
        copies.extend(copy_all([(branch.at[rows], branch_out.at[rows])], o_sem.at[pl.ds(i, 1)]))

    gather.run(use)
    gather.finish()
    for copy in copies:
        copy.wait()


def back_call(grads, residual, cotangent, gains, wo, wg):
    return pl.pallas_call(
        back_kernel,
        out_shape=(shape((OWN, D), F32), shape((LEN, D), BF), shape((LEN, 256), BF), shape((8, D), F32)),
        in_specs=[IN_VMEM] * 4 + [ANYWHERE] * 9,
        out_specs=(IN_VMEM, ANYWHERE, IN_VMEM, IN_VMEM),
        scratch_shapes=[
            pltpu.VMEM((2, D, 128), BF),
            pltpu.VMEM((2, D, 2 * PAD), BF),
            pltpu.VMEM((LEN, D), BF),
            *Scatter.scratch(),
            DMA((Gather.COPIES,)),
            DMA((Gather.COPIES,)),
            DMA((32,)),
            DMA((4,)),
        ],
        compiler_params=params(3),
        cost_estimate=cost(12 * 10**9, 60 * 2**20),
        name="back",
    )(grads, residual, cotangent, gains, *wo, *wg)


def attend_back_kernel(
    query, keys, values, attended_grad, log_sum, cos, sin_up, sin_down, lowest,
    projected_grad, bias_sum, kt, key_acc, value_acc,
):
    for s in range(2):
        kt[s] = keys[:, s * 128 : (s + 1) * 128].astype(F32).T.astype(BF)
    key_acc[...] = jnp.zeros_like(key_acc)
    value_acc[...] = jnp.zeros_like(value_acc)
    for block in range(LEN // QB):
        start, stop = window(block)
        rows = slice(block * QB, (block + 1) * QB)
        bias_t = mask_bias(lowest[:, rows], start, stop, block)
        for s in range(2):
            lanes = slice(s * 128, (s + 1) * 128)
            q, k, v = query[rows, lanes], keys[start:stop, lanes], values[start:stop, lanes]
            grad, k_t = attended_grad[rows, lanes], kt[s, :, start:stop]
            halves, key_sum, value_sum = [], None, None
            for head_id in range(2):
                mine = head_lanes(QB, head_id)
                q_one = jnp.where(mine, q, jnp.zeros_like(q))
                g_one = jnp.where(mine, grad, jnp.zeros_like(grad))
                index = s * 2 + head_id
                probs = jnp.exp(dot_nt(k, q_one) + bias_t - log_sum[index : index + 1, rows])
                prob_grad = dot_nt(v, g_one)
                inner = jnp.sum(probs * prob_grad, axis=0, keepdims=True)
                score_grad = (probs * (prob_grad - inner)).astype(BF)
                made = dot(k_t, score_grad)
                halves.append(made[head_id * HD : (head_id + 1) * HD])
                key_part = dot(score_grad, q_one)
                value_part = dot(probs.astype(BF), g_one)
                key_sum = key_part if key_sum is None else key_sum + key_part
                value_sum = value_part if value_sum is None else value_sum + value_part
            query_grad = jnp.concatenate(halves, axis=0).T * HD ** (-0.5)
            query_grad = roll_rotate(query_grad, cos[rows, :], -sin_up[rows, :], -sin_down[rows, :])
            projected_grad[rows, s * 384 : s * 384 + 128] = query_grad.astype(BF)
            key_acc[s, start:stop, :] += key_sum
            value_acc[s, start:stop, :] += value_sum
    for s in range(2):
        made = roll_rotate(key_acc[s], cos[...], -sin_up[...], -sin_down[...])
        projected_grad[:, s * 384 + 128 : s * 384 + 256] = made.astype(BF)
        projected_grad[:, s * 384 + 256 : s * 384 + 384] = value_acc[s].astype(BF)
    bias_sum[...] = jnp.broadcast_to(
        jnp.sum(projected_grad[...].astype(F32), axis=0, keepdims=True), bias_sum.shape
    )


def attend_back_call(query, keys, values, attended_grad, log_sum, cos, sin_up, sin_down, lowest):
    return pl.pallas_call(
        attend_back_kernel,
        out_shape=(shape((LEN, 768), BF), shape((8, 768), F32)),
        in_specs=[IN_VMEM] * 9,
        out_specs=(IN_VMEM, IN_VMEM),
        scratch_shapes=[
            pltpu.VMEM((2, 128, LEN), BF),
            pltpu.VMEM((2, LEN, 128), F32),
            pltpu.VMEM((2, LEN, 128), F32),
        ],
        compiler_params=params(),
        cost_estimate=cost(15 * 10**9, 12 * 2**20),
        name="attend_back",
    )(query, keys, values, attended_grad, log_sum, cos, sin_up, sin_down, lowest)


def close_kernel(projected_grad, hidden, tok, residual, residual_grad, gains, head, *rest):
    wd_in, (mixed, grad_tokens, norm_sums) = rest[0:5], rest[5:8]
    wv, wd = rest[8:10]
    a_refs, b_refs, (w_sem,) = rest[10:20], rest[20:30], rest[30:31]
    near = Near()
    pairs = []
    for k in range(4):
        for h in range(2):
            for s in range(2):
                row = pl.ds(pl.multiple_of(dp_of(k, h) * 256, 256), 256)
                pairs.append((head.at[k * 4 + h * 2 + s, pl.ds(0, 256)], wv.at[s, row]))
    head_copies = copy_all(pairs, w_sem.at[pl.ds(0, 16)])
    down_copies = copy_all(weight_pairs(wd_in, wd), w_sem.at[pl.ds(16, 16)])
    greet([near.dev["x"], near.dev["z"], near.dev["s"]])
    one, two = Scatter(near, a_refs), Scatter(near, b_refs)

    def make_one(chip):
        rows = chip_rows(chip)
        one.part[...] = dot_nt(projected_grad[rows, :384], wv[0]) + dot_nt(projected_grad[rows, 384:], wv[1])

    def make_two(chip):
        rows = chip_rows(chip)
        two.part[...] = dot_nt(hidden[rows, :PAD], wd[0]) + dot_nt(hidden[rows, PAD:], wd[1])

    for copy in head_copies:
        copy.wait()
    one.produce("d", make_one)
    one.produce("z", make_one)
    one.far()
    one.produce("x", make_one)
    one.z_direct()
    one.produce("o", make_one)
    one.x_direct()
    for copy in down_copies:
        copy.wait()
    two.produce("d", make_two)
    two.produce("z", make_two)
    one.relays()
    two.far()
    two.produce("x", make_two)
    two.z_direct()
    two.produce("o", make_two)
    two.x_direct()
    first, second = one.result()
    normed, inverse = layer_norm_parts(tok[...].astype(F32))
    part, gain_sum, shift_sum = norm_back(
        jnp.concatenate([first, second], axis=0), normed, inverse, gains[0:1, :]
    )
    grad_tokens[...] = residual_grad[...] + part
    norm_sums[0:1, :] = gain_sum
    norm_sums[1:2, :] = shift_sum
    two.relays()
    first, second = two.result()
    mixed[:HALF, :] = residual[:HALF, :] + first
    mixed[HALF:, :] = residual[HALF:, :] + second


def close_call(projected_grad, hidden, tokens, residual, residual_grad, gains, head, wd):
    return pl.pallas_call(
        close_kernel,
        out_shape=(shape((OWN, D), F32), shape((OWN, D), F32), shape((8, D), F32)),
        in_specs=[IN_VMEM] * 6 + [ANYWHERE] * 6,
        out_specs=(IN_VMEM,) * 3,
        scratch_shapes=[
            pltpu.VMEM((2, D, 384), BF),
            pltpu.VMEM((2, D, PAD), BF),
            *Scatter.scratch(),
            *Scatter.scratch(),
            DMA((32,)),
        ],
        compiler_params=params(4),
        cost_estimate=cost(10 * 10**9, 60 * 2**20),
        name="close",
    )(projected_grad, hidden, tokens, residual, residual_grad, gains, head, *wd)


def over_y(v, k):
    pairs = [(h * 4 + y, h * 4 + (y + k) % 4) for h in range(2) for y in range(4)]
    return lax.ppermute(v, "dp", pairs)


def over_x(v):
    return lax.ppermute(v, "dp", [(d, (d + 4) % 8) for d in range(8)])


def over_z(v):
    return lax.ppermute(v, "tensor", [(t, (3 - t // 4) * 4 + t % 4) for t in range(16)])


def y_last(base):
    return (base, over_y(base, 1), over_y(base, 2), over_y(base, 3))


def z_last(base):
    rings = y_last(base)
    return rings + (over_z(jnp.concatenate(rings, axis=0)),)


def around(v, axis, k):
    y = lax.axis_index("dp") % 4
    return lax.dynamic_index_in_dim(v, (y + k) % 4, axis, keepdims=False)


def sum_y(v):
    total = around(v, 1, 0).astype(F32)
    for k in (1, 2, 3):
        total = total + over_y(around(v, 1, k), k).astype(F32)
    return total


def sum_x(v):
    h = lax.axis_index("dp") // 4
    theirs = lax.dynamic_index_in_dim(v, 1 - h, 0, keepdims=False).astype(BF)
    mine = lax.dynamic_index_in_dim(v, h, 0, keepdims=False).astype(F32)
    return mine + over_x(theirs).astype(F32)


def tables(segments):
    z = lax.axis_index("tensor") // 4
    seg = lax.dynamic_index_in_dim(segments, z // 2, 0, keepdims=True)
    index = jnp.arange(LEN, dtype=jnp.int32)[None]
    before = jnp.concatenate([jnp.full((1, 1), -1, jnp.int32), seg[:, :-1]], axis=1)
    starts = lax.cummax(jnp.where(seg != before, index, 0), axis=1)
    lowest = jnp.maximum(starts, index - (WINDOW - 1))
    half_rot = ROT // 2
    inverse = jnp.exp(jnp.arange(half_rot, dtype=F32) * (-2.0 * math.log(BASE_FREQ) / ROT))
    angles = (index - starts).astype(F32) * inverse[:, None]
    cosine, sine = lax.optimization_barrier((jnp.cos(angles).T, jnp.sin(angles).T))
    none = jnp.zeros((LEN, half_rot), F32)
    rest = jnp.zeros((LEN, HD - ROT), F32)
    cos = jnp.concatenate([cosine, cosine, rest + 1.0] * 2, axis=1)
    sin_up = jnp.concatenate([-sine, none, rest] * 2, axis=1)
    sin_down = jnp.concatenate([none, sine, rest] * 2, axis=1)
    return cos, sin_up, sin_down, lowest


def wide(w):
    return jnp.pad(w, [(0, 0)] * (w.ndim - 1) + [(0, PAD - UNITS)])


def per_device(
    tokens,
    segments,
    first_gain,
    first_shift,
    heads_weight,
    heads_bias,
    output_weight,
    second_gain,
    second_shift,
    gate_up_weight,
    down_weight,
    cotangent,
):
    dp = lax.axis_index("dp")
    small = jnp.stack([first_gain, first_shift, second_gain, second_shift]).astype(BF).astype(F32)
    small = jnp.pad(small, [(0, 4), (0, 0)])
    here = (jnp.arange(8) == dp).astype(BF)[None, None, :, None]
    bias = (heads_bias.astype(BF)[:, :, None, :] * here).reshape(1, 384)
    head = jnp.concatenate([heads_weight.astype(BF).reshape(256, 384), jnp.pad(bias, [(0, 15), (0, 0)])], axis=0)

    out_t = output_weight.T.astype(BF)
    down_t = wide(down_weight.T.astype(BF))
    gate_up = wide(gate_up_weight.astype(BF)).reshape(256, 2 * PAD)
    gate_two = jnp.stack([gate_up, over_z(gate_up)])
    gate_four = jnp.concatenate([gate_two, over_x(gate_two)], axis=0)
    down_two = jnp.stack([down_t, over_x(down_t)])
    out_two = jnp.stack([out_t, over_x(out_t)])

    cos, sin_up, sin_down, lowest = tables(segments)
    first_all, cot_all, gains, head_all = open_call(tokens, cotangent, small, head)
    gate_four, down_two, out_two, first_all = lax.optimization_barrier((gate_four, down_two, out_two, first_all))
    wo = z_last(out_two)
    wg = y_last(gate_four)
    wd = z_last(down_two)

    query, keys, values, attended, log_sum = attend_call(first_all, head_all, cos, sin_up, sin_down, lowest)
    residual, second_all, hidden, grads = middle_call(attended, tokens, gains, cot_all, wo, wg, wd)

    grad_gate = dot_tn(second_all, grads).astype(BF).reshape(2, 4, 256, 4 * PAD)
    grad_down = dot_tn(cot_all, hidden).astype(BF).reshape(2, 4, 256, 2 * PAD)
    grad_gate = sum_y(grad_gate)
    grad_gate = grad_gate[..., : 2 * PAD] + over_z(grad_gate[..., 2 * PAD :].astype(BF)).astype(F32)
    grad_gate = sum_x(grad_gate)
    grad_down = grad_down[..., :PAD].astype(F32) + over_z(grad_down[..., PAD:]).astype(F32)
    grad_down = sum_x(sum_y(grad_down.astype(BF)))

    residual_grad, branch_all, attended_grad, sums_two = back_call(grads, residual, cotangent, gains, wo, wg)
    grad_out = dot_tn(branch_all, attended).astype(BF)
    projected_grad, bias_sum = attend_back_call(
        query, keys, values, attended_grad, log_sum, cos, sin_up, sin_down, lowest
    )
    grad_heads = dot_tn(first_all, projected_grad).astype(BF)
    bias_rows = jnp.pad(bias_sum[:1].astype(BF), [(0, 15), (0, 0)])
    parts = []
    for s in range(2):
        rows = jnp.concatenate(
            [grad_heads[:, s * 384 : (s + 1) * 384], grad_out[:, s * 128 : (s + 1) * 128]], axis=1
        ).reshape(2, 4, 256, 512)
        tail = jnp.pad(bias_rows[:, s * 384 : (s + 1) * 384], [(0, 0), (0, 128)])
        tail = jnp.broadcast_to(tail, (2, 4, 16, 512))
        parts.append(jnp.concatenate([rows, tail], axis=2))
    last = sum_y(jnp.concatenate(parts, axis=3))
    last = last[..., :512] + over_z(last[..., 512:].astype(BF)).astype(F32)
    last = sum_x(last)

    mixed, grad_tokens, sums_one = close_call(
        projected_grad, hidden, tokens, residual, residual_grad, gains, head_all, wd
    )
    norms = jnp.concatenate([sums_one[:2], sums_two[:2]], axis=0).reshape(64, 128)
    norms = lax.psum(norms, ("dp", "tensor")).reshape(4, D)
    place = dp * 256 + lax.axis_index("tensor") * 16
    norms = lax.dynamic_slice_in_dim(norms, place, 16, 1)

    grad_heads = last[:256, :384].reshape(256, 3, 128)
    grad_bias = lax.dynamic_slice_in_dim(last[256, :384].reshape(3, 2, HD), dp * 8, 8, 2)
    grad_output = last[:256, 384:].T
    grad_gate_up = grad_gate.reshape(256, 2, PAD)[..., :UNITS]
    grad_down = grad_down[:, :UNITS].T
    return (
        mixed,
        grad_tokens,
        norms[0],
        norms[1],
        grad_heads,
        grad_bias,
        grad_output,
        norms[2],
        norms[3],
        grad_gate_up,
        grad_down,
    )


ALL = ("dp", "tensor")


def solution(mesh):
    return jax.shard_map(
        per_device,
        mesh=mesh,
        in_specs=(
            P(ALL, None),
            P("dp", None),
            P("dp"),
            P("dp"),
            P("dp", None, "tensor"),
            P(None, "tensor", "dp"),
            P("tensor", "dp"),
            P("dp"),
            P("dp"),
            P("dp", None, "tensor"),
            P("tensor", "dp"),
            P(ALL, None),
        ),
        out_specs=(
            P(ALL, None),
            P(ALL, None),
            P(ALL),
            P(ALL),
            P("dp", None, "tensor"),
            P(None, "tensor", "dp"),
            P("tensor", "dp"),
            P(ALL),
            P(ALL),
            P("dp", None, "tensor"),
            P("tensor", "dp"),
        ),
        check_vma=False,
    )
```

time: 1890 us -> 653 us (0.35)
  waiting for transfers between devices: 1400 us -> 143 us
  Pallas kernels: 0 us -> 242 us
  matrix products: 130 us -> 23.6 us
  blocking collectives: 176 us -> 89.7 us
  starting transfers between devices: 1.17 us -> 58.1 us
  local copies, waits for them, and re-layouts: 99.9 us -> 53.4 us
  other arithmetic: 65.7 us -> 29.2 us
    unnamed x18 -> x0, waiting for transfers between devices: 638 us -> none
    reduce_scatter x8 -> x0, waiting for transfers between devices: 458 us -> none  [the longest x4 251 us: scatter_w(): return lax.psum_scatter(v, ('zhi', 'dp'), scatter_dimension=0, tiled=False)]
    all_gather x8 -> x0, waiting for transfers between devices: 299 us -> none  [the longest x4 235 us: gather_w(): return lax.all_gather(w, ('zhi', 'dp'), axis=0, tiled=False)]
    pallas_call x0 -> x6, Pallas kernels: none -> 242 us  [the longest x1 63.8 us: open_call(): pl.pallas_call(open_kernel, out_shape=(shape((LEN, D), BF), shape((LEN, D...]
    ppermute x0 -> x30, waiting for transfers between devices: none -> 143 us  [the longest x18 126 us: over_y(): return lax.ppermute(v, 'dp', pairs)]
    dot_general x18 -> x4, matrix products: 130 us -> 23.6 us  [dot_tn(): lax.dot_general(left, right, (((0,), (0,)), ((), ())), preferred_element_...]
    unnamed x1 -> x0, blocking collectives: 93.2 us -> none
    psum x0 -> x1, blocking collectives: none -> 89.7 us  [per_device(): norms = lax.psum(norms, ('dp', 'tensor')).reshape(4, D)]
  transfers between devices with their start and end apart: 17 -> 30, of which waited for: 14 -> 11; matrix products, arithmetic and copies ran while one was open for 11% -> 9% of each run, Pallas kernels for 0% -> 20%
where the time goes in v2:
time: 653 us; the launch traced here: 641 us
  Pallas kernels  242 us (37%)
  waiting for transfers between devices  143 us (22%)
  blocking collectives  89.7 us (14%)
  starting transfers between devices  58.1 us (9%)
  local copies, waits for them, and re-layouts  53.4 us (8%)
  other arithmetic  29.2 us (4%)
  matrix products  23.6 us (4%)
    ppermute x18, waiting for transfers between devices, over_y(): return lax.ppermute(v, 'dp', pairs)  126 us
    psum x1, blocking collectives, per_device(): norms = lax.psum(norms, ('dp', 'tensor')).reshape(4, D)  89.7 us
    pallas_call x1, Pallas kernels, open_call(): pl.pallas_call(open_kernel, out_shape=(shape((LEN, D), BF), shape((LEN, D...  63.8 us
    pallas_call x1, Pallas kernels, back_call(): pl.pallas_call(back_kernel, out_shape=(shape((OWN, D), F32), shape((LEN,...  50.9 us
    pallas_call x1, Pallas kernels, middle_call(): pl.pallas_call(middle_kernel, out_shape=(shape((OWN, D), F32), shape((LEN...  50.3 us
    pallas_call x1, Pallas kernels, close_call(): pl.pallas_call(close_kernel, out_shape=(shape((OWN, D), F32), shape((OWN,...  45.8 us
    ppermute x18, starting transfers between devices, over_y(): return lax.ppermute(v, 'dp', pairs)  27.5 us
    dot_general x4, matrix products, dot_tn(): lax.dot_general(left, right, (((0,), (0,)), ((), ())), preferred_element_...  23.6 us
  transfers between devices with their start and end apart: 30, of which 11 were waited for; matrix products, arithmetic and copies ran while one was open for 9% of the time, Pallas kernels for 20%

profile of v2, /device:TPU:0, one launch (start us, length us, event | category | flops | bytes accessed | tf_op | source)
XLA Modules:
  0.0 641.3 jit_solution(17161309165186762679)
XLA Ops:
  2.2 4.2 collective-permute-start
  10.6 4.9 collective-permute-done
  20.6 63.8 %open.1 = (bf16[1024,2048]{1,0:T(8,128)(2,1)}, bf16[1024,2048]{1,0:T(8,128)(2,1)}, f32[8,2048]{1,0:T(8,128)}, bf16[16,272,384]{2,1,0:T(8,128)(2,1)}) custom-call(bf16[128,2048]{1,0:T(8,128)(2,1)} %tok.5, bf16[128,2048]{1,0:T(8,128)(2,1)} %cot.3, f32[8,256]{1,0:T(8,128)} %fusion.23.small, bf16[272,384]{1,0:T(8,128)(2,1)} %fusion.13.head), custom_call_target="tpu_custom_call" | custom-call | flops 1000000000 | bytes 62914560 | tf_op jit(solution)/shard_map/open/pallas_call | solution.py:481
  96.5 11.7 %collective-permute-done.13.rest_12_.rest_3_ = bf16[2,256,384]{2,1,0:T(8,128)(2,1)S(1)} collective-permute-done((bf16[2,256,384]{2,1,0:T(8,128)(2,1)S(1)}, bf16[2,256,384]{2,1,0:T(8,128)(2,1)S(1)}, u32[]{:S(2)}, u32[]{:S(2)}) %collective-permute-start.13) | collective-permute-done | bytes 393248 | tf_op jit(solution)/shard_map/ppermute | solution.py:930
  108.2 3.8 collective-permute-start.6
  116.3 60.6 %collective-permute-done.6.rest_3_ = bf16[2,256,128]{2,1,0:T(8,128)(2,1)S(1)} collective-permute-done((bf16[2,256,128]{2,1,0:T(8,128)(2,1)S(1)}, bf16[2,256,128]{2,1,0:T(8,128)(2,1)S(1)}, u32[]{:S(2)}, u32[]{:S(2)}) %collective-permute-start.6) | collective-permute-done | bytes 131104 | tf_op jit(solution)/shard_map/ppermute | solution.py:930
  179.7 3.6 collective-permute-done.5.rest_2_
  186.3 3.7 collective-permute-done.4.rest_1_
  199.3 18.7 %attend.1 = (bf16[1024,256]{1,0:T(8,128)(2,1)}, bf16[1024,256]{1,0:T(8,128)(2,1)}, bf16[1024,256]{1,0:T(8,128)(2,1)}, bf16[1024,256]{1,0:T(8,128)(2,1)}, f32[8,1024]{1,0:T(8,128)}) custom-call(bf16[1024,2048]{1,0:T(8,128)(2,1)} %get-tuple-element.40.first, bf16[16,272,384]{2,1,0:T(8,128)(2,1)} %get-tuple-element.41.head, f32[1024,128]{1,0:T(8,128)} %concatenate.46.cos, ...), custom_call_target="tpu_custom_call" | custom-call | flops 5000000000 | bytes 12582912 | tf_op jit(solution)/shard_map/attend/pallas_call | solution.py:592
  218.2 50.3 %middle.1 = (f32[128,2048]{1,0:T(8,128)}, bf16[1024,2048]{1,0:T(8,128)(2,1)}, bf16[1024,768]{1,0:T(8,128)(2,1)}, bf16[1024,1536]{1,0:T(8,128)(2,1)}) custom-call(bf16[1024,256]{1,0:T(8,128)(2,1)} %get-tuple-element.47.attended, bf16[128,2048]{1,0:T(8,128)(2,1)} %tok.5, f32[8,2048]{1,0:T(8,128)} %get-tuple-element.48.gains, ...), custom_call_target="tpu_custom_call" | custom-call | flops 20000000000 | bytes 62914560 | tf_op jit(solution)/shard_map/middle/pallas_call | solution.py:691
  268.5 6.8 %convolution_convert_fusion.1 = bf16[2048,768]{1,0:T(8,128)(2,1)S(1)} fusion(bf16[1024,2048]{1,0:T(8,128)(2,1)} %get-tuple-element.49.cot_all, bf16[1024,768]{1,0:T(8,128)(2,1)} %get-tuple-element.58.hidden), kind=kOutput, calls=%fused_computation.2 | convolution fusion | flops 3222798336 | bytes 8912896 | tf_op jit(solution)/shard_map/dot_general | solution.py:286
  275.3 8.8 %convolution_convert_fusion = bf16[2048,1536]{1,0:T(8,128)(2,1)} fusion(bf16[1024,2048]{1,0:T(8,128)(2,1)S(1)} %copy-done.31, bf16[1024,1536]{1,0:T(8,128)(2,1)S(1)} %copy-done.32), kind=kOutput, calls=%fused_computation | convolution fusion | flops 6445596672 | bytes 13631488 | tf_op jit(solution)/shard_map/dot_general | solution.py:286
  284.1 50.9 %back.1 = (f32[128,2048]{1,0:T(8,128)}, bf16[1024,2048]{1,0:T(8,128)(2,1)}, bf16[1024,256]{1,0:T(8,128)(2,1)}, f32[8,2048]{1,0:T(8,128)}) custom-call(bf16[1024,1536]{1,0:T(8,128)(2,1)} %get-tuple-element.53.grads, f32[128,2048]{1,0:T(8,128)} %get-tuple-element.54.residual, bf16[128,2048]{1,0:T(8,128)(2,1)} %cot.3, f32[8,2048]{1,0:T(8,128)} %get-tuple-element.48.gains, ...), custom_call_target="tpu_custom_call" | custom-call | flops 12000000000 | bytes 62914560 | tf_op jit(solution)/shard_map/back/pallas_call | solution.py:768
  335.0 12.9 %attend_back.1 = (bf16[1024,768]{1,0:T(8,128)(2,1)}, f32[8,768]{1,0:T(8,128)}) custom-call(bf16[1024,256]{1,0:T(8,128)(2,1)} %get-tuple-element.44.query, bf16[1024,256]{1,0:T(8,128)(2,1)} %get-tuple-element.45.keys, bf16[1024,256]{1,0:T(8,128)(2,1)} %get-tuple-element.46.values, bf16[1024,256]{1,0:T(8,128)(2,1)} %get-tuple-element.55.attended_grad, ...), custom_call_target="tpu_custom_call" | custom-call | flops 15000000512 | bytes 12582912 | tf_op jit(solution)/shard_map/attend_back/pallas_call | solution.py:836
  347.9 6.2 convolution_convert_fusion.2
  372.0 4.5 reshape.183
  376.4 4.3 copy.89
  390.0 45.8 %close.1 = (f32[128,2048]{1,0:T(8,128)}, f32[128,2048]{1,0:T(8,128)}, f32[8,2048]{1,0:T(8,128)}) custom-call(bf16[1024,768]{1,0:T(8,128)(2,1)} %get-tuple-element.57.projected_grad, bf16[1024,768]{1,0:T(8,128)(2,1)} %get-tuple-element.58.hidden, bf16[128,2048]{1,0:T(8,128)(2,1)} %tok.5, f32[128,2048]{1,0:T(8,128)} %get-tuple-element.54.residual, ...), custom_call_target="tpu_custom_call" | custom-call | flops 10000000000 | bytes 62914560 | tf_op jit(solution)/shard_map/close/pallas_call | solution.py:910
  437.5 4.7 dynamic-slice_bitcast_fusion.2
  443.7 89.7 %psum.7 = f32[4,2048]{1,0:T(4,128)S(1)} all-reduce(f32[4,2048]{1,0:T(4,128)S(1)} %pad_maximum_fusion.8), channel_id=1, replica_groups=mesh['dp'=8,'tensor'=16] {'dp','tensor'}, use_global_device_ids=true, to_apply=%region_2.3 | all-reduce | flops 8192 | bytes 65536 | tf_op jit(solution)/shard_map/psum | solution.py:1062
  548.4 6.5 %collective-permute-done.18 = bf16[2,272,512]{2,1,0:T(8,128)(2,1)S(1)} collective-permute-done((bf16[2,272,512]{2,1,0:T(8,128)(2,1)S(1)}, bf16[2,272,512]{2,1,0:T(8,128)(2,1)S(1)}, u32[]{:S(2)}, u32[]{:S(2)}) %collective-permute-start.18) | collective-permute-done | bytes 557088 | tf_op jit(solution)/shard_map/ppermute | solution.py:938
  557.4 46.0 %collective-permute-done.22 = bf16[2,256,1536]{2,1,0:T(8,128)(2,1)} collective-permute-done((bf16[2,256,1536]{2,1,0:T(8,128)(2,1)}, bf16[2,256,1536]{2,1,0:T(8,128)(2,1)}, u32[]{:S(2)}, u32[]{:S(2)}) %collective-permute-start.22) | collective-permute-done | bytes 1572896 | tf_op jit(solution)/shard_map/ppermute | solution.py:930
  615.0 8.4 %collective-permute-start.29 = (bf16[256,384]{0,1:T(8,128)(2,1)S(1)}, bf16[256,384]{0,1:T(8,128)(2,1)}, u32[]{:S(2)}, u32[]{:S(2)}) collective-permute-start(bf16[256,384]{0,1:T(8,128)(2,1)S(1)} %fusion.14), channel_id=1, source_target_pairs={{0,64},{16,80},{32,96},{48,112},{64,0},{80,16},{96,32},{112,48},{1... | collective-permute-start | bytes 589832 | tf_op jit(solution)/shard_map/ppermute | solution.py:934
  632.7 4.2 collective-permute-done.24
  (212 shorter events, 114.5 us)
Async XLA Ops:
  6.5 78.0 %collective-permute-start.3 = (bf16[256,128]{1,0:T(8,128)(2,1)S(1)}, bf16[256,128]{1,0:T(8,128)(2,1)S(1)}, u32[]{:S(2)}, u32[]{:S(2)}) collective-permute-start(bf16[256,128]{1,0:T(8,128)(2,1)S(1)} %bitcast.110), channel_id=1, source_target_pairs={{0,64},{16,80},{32,96},{48,112},{64,0},{80,16},{96,32},{112,48},{1... | collective-permute-start | bytes 196616 | tf_op jit(solution)/shard_map/ppermute | solution.py:934
  9.8 74.7 %collective-permute-start.2 = (bf16[256,384]{1,0:T(8,128)(2,1)S(1)}, bf16[256,384]{1,0:T(8,128)(2,1)S(1)}, u32[]{:S(2)}, u32[]{:S(2)}) collective-permute-start(bf16[256,384]{1,0:T(8,128)(2,1)S(1)} %get-tuple-element.127), channel_id=1, source_target_pairs={{0,64},{16,80},{32,96},{48,112},{64,0},{80,16},{96,32},{112,48},{1... | collective-permute-start | bytes 589832 | tf_op jit(solution)/shard_map/ppermute | solution.py:934
  15.5 69.0 %collective-permute-start.1 = (bf16[2,256,768]{2,1,0:T(8,128)(2,1)S(1)}, bf16[2,256,768]{2,1,0:T(8,128)(2,1)}, u32[]{:S(2)}, u32[]{:S(2)}) collective-permute-start(bf16[2,256,768]{2,1,0:T(8,128)(2,1)S(1)} %pad_maximum_fusion.4), channel_id=1, source_target_pairs={{0,64},{16,80},{32,96},{48,112},{64,0},{80,16},{96,32},{112,48},{1... | collective-permute-start | bytes 2359304 | tf_op jit(solution)/shard_map/ppermute | solution.py:934
  87.1 21.0 %collective-permute-start.13 = (bf16[2,256,384]{2,1,0:T(8,128)(2,1)S(1)}, bf16[2,256,384]{2,1,0:T(8,128)(2,1)S(1)}, u32[]{:S(2)}, u32[]{:S(2)}) collective-permute-start(bf16[2,256,384]{2,1,0:T(8,128)(2,1)S(1)} %pad_maximum_fusion.6.rest_9_.rest_0_), channel_id=1, source_target_pairs={{0,48},{16,0},{32,16},{48,32},{64,112},{80,64},{96,80},{112,96},{1... | collective-permute-start | bytes 1179656 | tf_op jit(solution)/shard_map/ppermute | solution.py:930
  90.2 18.0 %collective-permute-start.12 = (bf16[2,256,384]{2,1,0:T(8,128)(2,1)S(1)}, bf16[2,256,384]{2,1,0:T(8,128)(2,1)S(1)}, u32[]{:S(2)}, u32[]{:S(2)}) collective-permute-start(bf16[2,256,384]{2,1,0:T(8,128)(2,1)S(1)} %pad_maximum_fusion.6.rest_9_.rest_0_), channel_id=1, source_target_pairs={{0,32},{16,48},{32,0},{48,16},{64,96},{80,112},{96,64},{112,80},{1... | collective-permute-start | bytes 1179656 | tf_op jit(solution)/shard_map/ppermute | solution.py:930
  90.8 21.4 %collective-permute-start.11 = (bf16[2,256,384]{2,1,0:T(8,128)(2,1)S(1)}, bf16[2,256,384]{2,1,0:T(8,128)(2,1)S(1)}, u32[]{:S(2)}, u32[]{:S(2)}) collective-permute-start(bf16[2,256,384]{2,1,0:T(8,128)(2,1)S(1)} %pad_maximum_fusion.6.rest_9_.rest_0_), channel_id=1, source_target_pairs={{0,16},{16,32},{32,48},{48,0},{64,80},{80,96},{96,112},{112,64},{1... | collective-permute-start | bytes 1179656 | tf_op jit(solution)/shard_map/ppermute | solution.py:930
  92.5 125.6 %collective-permute-start.10 = (bf16[4,256,768]{2,1,0:T(8,128)(2,1)}, bf16[4,256,768]{2,1,0:T(8,128)(2,1)}, u32[]{:S(2)}, u32[]{:S(2)}) collective-permute-start(bf16[4,256,768]{2,1,0:T(8,128)(2,1)} %pad_maximum_fusion.2.rest_5_), channel_id=1, source_target_pairs={{0,48},{16,0},{32,16},{48,32},{64,112},{80,64},{96,80},{112,96},{1... | collective-permute-start | bytes 4718600 | tf_op jit(solution)/shard_map/ppermute | solution.py:930
  94.8 123.3 %collective-permute-start.9 = (bf16[4,256,768]{2,1,0:T(8,128)(2,1)}, bf16[4,256,768]{2,1,0:T(8,128)(2,1)}, u32[]{:S(2)}, u32[]{:S(2)}) collective-permute-start(bf16[4,256,768]{2,1,0:T(8,128)(2,1)} %pad_maximum_fusion.2.rest_5_), channel_id=1, source_target_pairs={{0,32},{16,48},{32,0},{48,16},{64,96},{80,112},{96,64},{112,80},{1... | collective-permute-start | bytes 4718600 | tf_op jit(solution)/shard_map/ppermute | solution.py:930
  108.2 110.0 %collective-permute-start.8 = (bf16[4,256,768]{2,1,0:T(8,128)(2,1)}, bf16[4,256,768]{2,1,0:T(8,128)(2,1)}, u32[]{:S(2)}, u32[]{:S(2)}) collective-permute-start(bf16[4,256,768]{2,1,0:T(8,128)(2,1)} %pad_maximum_fusion.2.rest_5_), channel_id=1, source_target_pairs={{0,16},{16,32},{32,48},{48,0},{64,80},{80,96},{96,112},{112,64},{1... | collective-permute-start | bytes 4718600 | tf_op jit(solution)/shard_map/ppermute | solution.py:930
  108.2 68.7 %collective-permute-start.6 = (bf16[2,256,128]{2,1,0:T(8,128)(2,1)S(1)}, bf16[2,256,128]{2,1,0:T(8,128)(2,1)S(1)}, u32[]{:S(2)}, u32[]{:S(2)}) collective-permute-start(bf16[2,256,128]{2,1,0:T(8,128)(2,1)S(1)} %pad_maximum_fusion.7.rest_0_), channel_id=1, source_target_pairs={{0,48},{16,0},{32,16},{48,32},{64,112},{80,64},{96,80},{112,96},{1... | collective-permute-start | bytes 393224 | tf_op jit(solution)/shard_map/ppermute | solution.py:930
  113.7 104.5 %collective-permute-start.14 = (bf16[8,256,384]{2,1,0:T(8,128)(2,1)}, bf16[8,256,384]{2,1,0:T(8,128)(2,1)}, u32[]{:S(2)}, u32[]{:S(2)}) collective-permute-start(bf16[8,256,384]{2,1,0:T(8,128)(2,1)} %pad_maximum_fusion.3), channel_id=1, source_target_pairs={{0,12},{1,13},{2,14},{3,15},{4,8},{5,9},{6,10},{7,11},{8,4},{9,5},... | collective-permute-start | bytes 4718600 | tf_op jit(solution)/shard_map/ppermute | solution.py:938
  190.1 28.0 %collective-permute-start.7 = (bf16[8,256,128]{2,1,0:T(8,128)(2,1)S(1)}, bf16[8,256,128]{2,1,0:T(8,128)(2,1)}, u32[]{:S(2)}, u32[]{:S(2)}) collective-permute-start(bf16[8,256,128]{2,1,0:T(8,128)(2,1)S(1)} %pad_maximum_fusion.5), channel_id=1, source_target_pairs={{0,12},{1,13},{2,14},{3,15},{4,8},{5,9},{6,10},{7,11},{8,4},{9,5},... | collective-permute-start | bytes 1572872 | tf_op jit(solution)/shard_map/ppermute | solution.py:938
  371.3 173.1 %collective-permute-start.25 = (bf16[2,4,256,384]{2,3,0,1:T(8,128)(2,1)}, bf16[2,4,256,384]{2,3,0,1:T(8,128)(2,1)}, u32[]{:S(2)}, u32[]{:S(2)}) collective-permute-start(bf16[2,4,256,384]{2,3,0,1:T(8,128)(2,1)} %copy.99), channel_id=1, source_target_pairs={{0,12},{1,13},{2,14},{3,15},{4,8},{5,9},{6,10},{7,11},{8,4},{9,5},... | collective-permute-start | bytes 4718600 | tf_op jit(solution)/shard_map/ppermute | solution.py:938
  386.5 146.9 %collective-permute-start.15 = (bf16[2,272,1024]{2,1,0:T(8,128)(2,1)}, bf16[2,272,1024]{2,1,0:T(8,128)(2,1)S(1)}, u32[]{:S(2)}, u32[]{:S(2)}) collective-permute-start(bf16[2,272,1024]{2,1,0:T(8,128)(2,1)} %get-tuple-element.114), channel_id=1, source_target_pairs={{0,16},{16,32},{32,48},{48,0},{64,80},{80,96},{96,112},{112,64},{1... | collective-permute-start | bytes 3342344 | tf_op jit(solution)/shard_map/ppermute | solution.py:930
  386.5 148.5 %collective-permute-start.17 = (bf16[2,272,1024]{2,1,0:T(8,128)(2,1)}, bf16[2,272,1024]{2,1,0:T(8,128)(2,1)S(1)}, u32[]{:S(2)}, u32[]{:S(2)}) collective-permute-start(bf16[2,272,1024]{2,1,0:T(8,128)(2,1)} %get-tuple-element.115), channel_id=1, source_target_pairs={{0,48},{16,0},{32,16},{48,32},{64,112},{80,64},{96,80},{112,96},{1... | collective-permute-start | bytes 3342344 | tf_op jit(solution)/shard_map/ppermute | solution.py:930
  389.8 147.3 %collective-permute-start.16 = (bf16[2,272,1024]{2,1,0:T(8,128)(2,1)S(1)}, bf16[2,272,1024]{2,1,0:T(8,128)(2,1)}, u32[]{:S(2)}, u32[]{:S(2)}) collective-permute-start(bf16[2,272,1024]{2,1,0:T(8,128)(2,1)S(1)} %get-tuple-element.116), channel_id=1, source_target_pairs={{0,32},{16,48},{32,0},{48,16},{64,96},{80,112},{96,64},{112,80},{1... | collective-permute-start | bytes 3342344 | tf_op jit(solution)/shard_map/ppermute | solution.py:930
  442.3 114.2 %collective-permute-start.20 = (bf16[2,256,1536]{2,1,0:T(8,128)(2,1)}, bf16[2,256,1536]{2,1,0:T(8,128)(2,1)}, u32[]{:S(2)}, u32[]{:S(2)}) collective-permute-start(bf16[2,256,1536]{2,1,0:T(8,128)(2,1)} %get-tuple-element.111), channel_id=1, source_target_pairs={{0,16},{16,32},{32,48},{48,0},{64,80},{80,96},{96,112},{112,64},{1... | collective-permute-start | bytes 4718600 | tf_op jit(solution)/shard_map/ppermute | solution.py:930
  533.4 70.0 %collective-permute-start.22 = (bf16[2,256,1536]{2,1,0:T(8,128)(2,1)}, bf16[2,256,1536]{2,1,0:T(8,128)(2,1)}, u32[]{:S(2)}, u32[]{:S(2)}) collective-permute-start(bf16[2,256,1536]{2,1,0:T(8,128)(2,1)} %get-tuple-element.112), channel_id=1, source_target_pairs={{0,48},{16,0},{32,16},{48,32},{64,112},{80,64},{96,80},{112,96},{1... | collective-permute-start | bytes 4718600 | tf_op jit(solution)/shard_map/ppermute | solution.py:930
  535.0 70.8 %collective-permute-start.21 = (bf16[2,256,1536]{2,1,0:T(8,128)(2,1)}, bf16[2,256,1536]{2,1,0:T(8,128)(2,1)}, u32[]{:S(2)}, u32[]{:S(2)}) collective-permute-start(bf16[2,256,1536]{2,1,0:T(8,128)(2,1)} %get-tuple-element.113), channel_id=1, source_target_pairs={{0,32},{16,48},{32,0},{48,16},{64,96},{80,112},{96,64},{112,80},{1... | collective-permute-start | bytes 4718600 | tf_op jit(solution)/shard_map/ppermute | solution.py:930
  540.0 14.9 %collective-permute-start.18 = (bf16[2,272,512]{2,1,0:T(8,128)(2,1)S(1)}, bf16[2,272,512]{2,1,0:T(8,128)(2,1)S(1)}, u32[]{:S(2)}, u32[]{:S(2)}) collective-permute-start(bf16[2,272,512]{2,1,0:T(8,128)(2,1)S(1)} %slice.151), channel_id=1, source_target_pairs={{0,12},{1,13},{2,14},{3,15},{4,8},{5,9},{6,10},{7,11},{8,4},{9,5},... | collective-permute-start | bytes 1671176 | tf_op jit(solution)/shard_map/ppermute | solution.py:938
  547.8 65.6 %collective-permute-start.26 = (bf16[2,256,384]{1,2,0:T(8,128)(2,1)}, bf16[2,256,384]{1,2,0:T(8,128)(2,1)}, u32[]{:S(2)}, u32[]{:S(2)}) collective-permute-start(bf16[2,256,384]{1,2,0:T(8,128)(2,1)} %get-tuple-element.121), channel_id=1, source_target_pairs={{0,16},{16,32},{32,48},{48,0},{64,80},{80,96},{96,112},{112,64},{1... | collective-permute-start | bytes 1179656 | tf_op jit(solution)/shard_map/ppermute | solution.py:930
  554.9 58.5 %collective-permute-start.28 = (bf16[2,256,384]{1,2,0:T(8,128)(2,1)}, bf16[2,256,384]{1,2,0:T(8,128)(2,1)}, u32[]{:S(2)}, u32[]{:S(2)}) collective-permute-start(bf16[2,256,384]{1,2,0:T(8,128)(2,1)} %get-tuple-element.122), channel_id=1, source_target_pairs={{0,48},{16,0},{32,16},{48,32},{64,112},{80,64},{96,80},{112,96},{1... | collective-permute-start | bytes 1179656 | tf_op jit(solution)/shard_map/ppermute | solution.py:930
  556.5 56.9 %collective-permute-start.27 = (bf16[2,256,384]{1,2,0:T(8,128)(2,1)}, bf16[2,256,384]{1,2,0:T(8,128)(2,1)}, u32[]{:S(2)}, u32[]{:S(2)}) collective-permute-start(bf16[2,256,384]{1,2,0:T(8,128)(2,1)} %get-tuple-element.123), channel_id=1, source_target_pairs={{0,32},{16,48},{32,0},{48,16},{64,96},{80,112},{96,64},{112,80},{1... | collective-permute-start | bytes 1179656 | tf_op jit(solution)/shard_map/ppermute | solution.py:930
  615.0 15.9 %collective-permute-start.29 = (bf16[256,384]{0,1:T(8,128)(2,1)S(1)}, bf16[256,384]{0,1:T(8,128)(2,1)}, u32[]{:S(2)}, u32[]{:S(2)}) collective-permute-start(bf16[256,384]{0,1:T(8,128)(2,1)S(1)} %fusion.14), channel_id=1, source_target_pairs={{0,64},{16,80},{32,96},{48,112},{64,0},{80,16},{96,32},{112,48},{1... | collective-permute-start | bytes 589832 | tf_op jit(solution)/shard_map/ppermute | solution.py:934
  (39 other events, 646.0 us)
